TPU v7x, 32 devices: a whole 2x2x4 slice. The times are simulated.
32 devices in a mesh: pipe: 2 (over x), row: 8 (over z, core), col: 2 (over y).
Axes of the slice: x: 2, y: 2, z: 4, core: 2. Of those that a mesh axis runs over, the one named last changes fastest.
Arguments:
- inputs: bfloat16 [4, 8, 1024, 512], P(None, 'row', 'col'), may hold values from -6 to 6
- first_gain: float32 [2, 512], P('pipe'), may hold values from 0.5 to 1.5
- first_shift: float32 [2, 512], P('pipe'), may hold values from -1.75 to 1.75
- qkv_weight: bfloat16 [2, 3, 512, 512], P('pipe', None, 'row', 'col'), may hold values from -0.25 to 0.25
- query_bias: float32 [2, 512], P('pipe', 'col'), may hold values from -3 to 3
- value_bias: float32 [2, 512], P('pipe', 'col'), may hold values from -1.75 to 1.75
- proj_weight: bfloat16 [2, 512, 512], P('pipe', 'col', 'row'), may hold values from -1 to 1
- proj_bias: float32 [2, 512], P('pipe'), may hold values from -1.75 to 1.75
- second_gain: float32 [2, 512], P('pipe'), may hold values from 0.5 to 1.5
- second_shift: float32 [2, 512], P('pipe'), may hold values from -1.75 to 1.75
- up_weight: bfloat16 [2, 512, 2048], P('pipe', 'row', 'col'), may hold values from -0.25 to 0.25
- up_bias: float32 [2, 2048], P('pipe', 'col'), may hold values from -3 to 3
- down_weight: bfloat16 [2, 2048, 512], P('pipe', 'col', 'row'), may hold values from -0.125 to 0.125
- down_bias: float32 [2, 512], P('pipe'), may hold values from -1.75 to 1.75
- cotangent: bfloat16 [4, 8, 1024, 512], P(None, 'row', 'col'), may hold values from -6 to 6
- live_clips: int32 [4, 8], P(None, 'row'), may hold values 0 or 1
Outputs:
- states: bfloat16 [2, 4, 8, 1024, 512], P('pipe', None, 'row', 'col')
- state_grads: float32 [2, 4, 8, 1024, 512], P('pipe', None, 'row', 'col')
- grad_first_gain: float32 [2, 512], P('pipe')
- grad_first_shift: float32 [2, 512], P('pipe')
- grad_qkv_weight: float32 [2, 3, 512, 512], P('pipe', None, 'row', 'col')
- grad_query_bias: float32 [2, 512], P('pipe', 'col')
- grad_value_bias: float32 [2, 512], P('pipe', 'col')
- grad_proj_weight: float32 [2, 512, 512], P('pipe', 'col', 'row')
- grad_proj_bias: float32 [2, 512], P('pipe')
- grad_second_gain: float32 [2, 512], P('pipe')
- grad_second_shift: float32 [2, 512], P('pipe')
- grad_up_weight: float32 [2, 512, 2048], P('pipe', 'row', 'col')
- grad_up_bias: float32 [2, 2048], P('pipe', 'col')
- grad_down_weight: float32 [2, 2048, 512], P('pipe', 'col', 'row')
- grad_down_bias: float32 [2, 512], P('pipe')
All inputs are finite; a program needn't handle non-finite values. No bound on the sum of `live_clips` on one device may be relied on, other than what follows from the above.
Results may differ from a plain program's by a relative error of at most 0.015.
Values may be sent and summed in bfloat16 or wider, within the bound.
A program may use at most 192 MiB of HBM per device.

v0:
```python
import math

import jax
import jax.numpy as jnp
from jax import lax
from jax.experimental import pallas as pl
from jax.experimental.pallas import tpu as pltpu
from jax.sharding import PartitionSpec as P

HD = 64


epsilon = 1e-05


def from_behind(value, axis, steps):
    count = lax.axis_size(axis)
    first, last = (max(0, -steps), min(count, count - steps))
    return lax.ppermute(value, axis, [(source, source + steps) for source in range(first, last)])


def exact_gelu(values):
    return jax.nn.gelu(values, approximate=False)


def spread_features(normed):
    return lax.all_gather(normed, "col", axis=0, tiled=True)


def sum_columns(partial_rows):
    return lax.psum_scatter(partial_rows, "col", scatter_dimension=0, tiled=True)


def spread_grads(grad_low):
    return lax.all_gather(grad_low, "col", axis=0, tiled=True)


def sum_grad_columns(partial_rows):
    return lax.psum_scatter(partial_rows, "col", scatter_dimension=0, tiled=True)


def norm_forward(values, gain, shift):
    row_mean = jnp.mean(values, axis=-1, keepdims=True)
    row_var = jnp.mean(jnp.square(values - row_mean), axis=-1, keepdims=True)
    inv_std = lax.rsqrt(row_var + epsilon)
    centered = (values - row_mean) * inv_std
    return (centered, inv_std[:, 0], (centered * gain + shift).astype(jnp.bfloat16))


def norm_backward(grad_norm, centered, inv_std, gain):
    grad_gain = jnp.sum(grad_norm * centered, axis=0)
    grad_shift = jnp.sum(grad_norm, axis=0)
    scaled = grad_norm * gain
    first = jnp.mean(scaled, axis=-1, keepdims=True)
    second = jnp.mean(scaled * centered, axis=-1, keepdims=True)
    grad_in = inv_std[:, None] * (scaled - first - centered * second)
    return (grad_in, grad_gain, grad_shift)


def attention_probs(query_heads, key_heads):
    score_scale = 1.0 / math.sqrt(HD)
    scores = (
        jnp.einsum("qhd,khd->hqk", query_heads, key_heads, preferred_element_type=jnp.float32)
        * score_scale
    )
    return jax.nn.softmax(scores, axis=-1)


def layer_forward(values, weights, params):
    qkv_full, proj_full, up_full, down_full = weights
    (
        gain_one,
        shift_one,
        query_bias,
        value_bias,
        proj_bias,
        gain_two,
        shift_two,
        up_bias,
        down_bias,
    ) = params
    head_count = qkv_full.shape[2] // HD
    centered_one, inv_one, normed_one = norm_forward(values, gain_one, shift_one)
    attn_input = spread_features(normed_one)
    frame_count = attn_input.shape[0]
    projected = jnp.einsum("sd,jde->jse", attn_input, qkv_full, preferred_element_type=jnp.float32)
    query_heads = (
        (projected[0] + query_bias).astype(jnp.bfloat16).reshape(frame_count, head_count, HD)
    )
    key_heads = projected[1].astype(jnp.bfloat16).reshape(frame_count, head_count, HD)
    value_heads = (
        (projected[2] + value_bias).astype(jnp.bfloat16).reshape(frame_count, head_count, HD)
    )
    softmax_out = attention_probs(query_heads, key_heads)
    context = jnp.einsum(
        "hqk,khd->qhd",
        softmax_out.astype(jnp.bfloat16),
        value_heads,
        preferred_element_type=jnp.float32,
    )
    context = context.reshape(frame_count, head_count * HD).astype(jnp.bfloat16)
    attended = (
        sum_columns(jnp.dot(context, proj_full, preferred_element_type=jnp.float32)) + proj_bias
    )
    hidden = values + attended
    centered_two, inv_two, normed_two = norm_forward(hidden, gain_two, shift_two)
    mlp_input = spread_features(normed_two)
    pre_act = jnp.dot(mlp_input, up_full, preferred_element_type=jnp.float32) + up_bias
    activated = exact_gelu(pre_act).astype(jnp.bfloat16)
    output = (
        hidden
        + sum_columns(jnp.dot(activated, down_full, preferred_element_type=jnp.float32))
        + down_bias
    )
    kept = (
        centered_one,
        inv_one,
        attn_input,
        query_heads,
        key_heads,
        value_heads,
        context,
        centered_two,
        inv_two,
        mlp_input,
        pre_act,
        activated,
    )
    return (output, kept)


def layer_backward(grad_out, kept, weights, params):
    qkv_full, proj_full, up_full, down_full = weights
    (
        gain_one,
        shift_one,
        query_bias,
        value_bias,
        proj_bias,
        gain_two,
        shift_two,
        up_bias,
        down_bias,
    ) = params
    (
        centered_one,
        inv_one,
        attn_input,
        query_heads,
        key_heads,
        value_heads,
        context,
        centered_two,
        inv_two,
        mlp_input,
        pre_act,
        activated,
    ) = kept
    frame_count = attn_input.shape[0]
    score_scale = 1.0 / math.sqrt(HD)
    grad_down_bias = jnp.sum(grad_out, axis=0)
    down_grad = spread_grads(grad_out.astype(jnp.bfloat16))
    grad_down = jnp.einsum("sf,sd->fd", activated, down_grad, preferred_element_type=jnp.float32)
    grad_act = jnp.einsum("sd,fd->sf", down_grad, down_full, preferred_element_type=jnp.float32)
    unused, gelu_pull = jax.vjp(exact_gelu, pre_act)
    grad_pre = gelu_pull(grad_act)[0]
    grad_up_bias = jnp.sum(grad_pre, axis=0)
    grad_pre_low = grad_pre.astype(jnp.bfloat16)
    grad_up = jnp.einsum("sd,sf->df", mlp_input, grad_pre_low, preferred_element_type=jnp.float32)
    grad_normed_two = sum_grad_columns(
        jnp.einsum("sf,df->sd", grad_pre_low, up_full, preferred_element_type=jnp.float32)
    )
    grad_hidden_norm, grad_gain_two, grad_shift_two = norm_backward(
        grad_normed_two, centered_two, inv_two, gain_two
    )
    grad_hidden = grad_out + grad_hidden_norm
    grad_proj_bias = jnp.sum(grad_hidden, axis=0)
    proj_grad = spread_grads(grad_hidden.astype(jnp.bfloat16))
    grad_proj = jnp.einsum("se,sd->ed", context, proj_grad, preferred_element_type=jnp.float32)
    grad_context = jnp.einsum("sd,ed->se", proj_grad, proj_full, preferred_element_type=jnp.float32)
    grad_context = grad_context.astype(jnp.bfloat16).reshape(query_heads.shape)
    softmax_out = attention_probs(query_heads, key_heads)
    grad_probs = jnp.einsum(
        "qhd,khd->hqk", grad_context, value_heads, preferred_element_type=jnp.float32
    )
    grad_value = jnp.einsum(
        "hqk,qhd->khd",
        softmax_out.astype(jnp.bfloat16),
        grad_context,
        preferred_element_type=jnp.float32,
    )
    grad_scores = softmax_out * (
        grad_probs - jnp.sum(softmax_out * grad_probs, axis=-1, keepdims=True)
    )
    scores_low = grad_scores.astype(jnp.bfloat16)
    grad_query = (
        jnp.einsum("hqk,khd->qhd", scores_low, key_heads, preferred_element_type=jnp.float32)
        * score_scale
    )
    grad_key = (
        jnp.einsum("hqk,qhd->khd", scores_low, query_heads, preferred_element_type=jnp.float32)
        * score_scale
    )
    grad_query = grad_query.reshape(frame_count, -1)
    grad_key = grad_key.reshape(frame_count, -1)
    grad_value = grad_value.reshape(frame_count, -1)
    grad_query_bias = jnp.sum(grad_query, axis=0)
    grad_value_bias = jnp.sum(grad_value, axis=0)
    grad_qkv_low = jnp.stack([grad_query, grad_key, grad_value]).astype(jnp.bfloat16)
    grad_qkv = jnp.einsum(
        "sd,jse->jde", attn_input, grad_qkv_low, preferred_element_type=jnp.float32
    )
    grad_normed_one = sum_grad_columns(
        jnp.einsum("jse,jde->sd", grad_qkv_low, qkv_full, preferred_element_type=jnp.float32)
    )
    grad_in_norm, grad_gain_one, grad_shift_one = norm_backward(
        grad_normed_one, centered_one, inv_one, gain_one
    )
    grad_in = grad_hidden + grad_in_norm
    weight_grads = (grad_qkv, grad_proj, grad_up, grad_down)
    vector_grads = (
        grad_gain_one,
        grad_shift_one,
        grad_query_bias,
        grad_value_bias,
        grad_proj_bias,
        grad_gain_two,
        grad_shift_two,
        grad_up_bias,
        grad_down_bias,
    )
    return (grad_in, weight_grads, vector_grads)


def store_slot(buffer, slot_index, is_valid, value):
    current = lax.dynamic_index_in_dim(buffer, slot_index, 0, keepdims=False)
    return lax.dynamic_update_index_in_dim(
        buffer, jnp.where(is_valid, value, current), slot_index, 0
    )


def reduce_end(weight_acc):
    return (
        lax.psum_scatter(
            weight_acc[0].astype(jnp.bfloat16), "row", scatter_dimension=1, tiled=True
        ).astype(jnp.float32),
        lax.psum_scatter(
            weight_acc[1].astype(jnp.bfloat16), "row", scatter_dimension=1, tiled=True
        ).astype(jnp.float32),
        lax.psum_scatter(
            weight_acc[2].astype(jnp.bfloat16), "row", scatter_dimension=0, tiled=True
        ).astype(jnp.float32),
        lax.psum_scatter(
            weight_acc[3].astype(jnp.bfloat16), "row", scatter_dimension=1, tiled=True
        ).astype(jnp.float32),
    )


def on_device(
    inputs,
    first_gain,
    first_shift,
    qkv_weight,
    query_bias,
    value_bias,
    proj_weight,
    proj_bias,
    second_gain,
    second_shift,
    up_weight,
    up_bias,
    down_weight,
    down_bias,
    cotangent,
    live_clips,
):
    micro_count = inputs.shape[0]
    row_count = inputs.shape[2]
    feature_count = inputs.shape[3]
    section_index = lax.axis_index("pipe")
    weights = (
        lax.all_gather(qkv_weight[0], "row", axis=1, tiled=True),
        lax.all_gather(proj_weight[0], "row", axis=1, tiled=True),
        lax.all_gather(up_weight[0], "row", axis=0, tiled=True),
        lax.all_gather(down_weight[0], "row", axis=1, tiled=True),
    )
    params = (
        first_gain[0],
        first_shift[0],
        query_bias[0],
        value_bias[0],
        proj_bias[0],
        second_gain[0],
        second_shift[0],
        up_bias[0],
        down_bias[0],
    )
    kept_buffers = ()
    zero_rows = jnp.zeros((row_count, feature_count), jnp.bfloat16)
    zero_stack = jnp.zeros((micro_count, row_count, feature_count), jnp.bfloat16)
    own_inputs = inputs[:, 0]

    def forward_tick(state_carry, tick_index):
        received, outputs, layer_inputs, buffers = state_carry
        batch_index = tick_index - section_index
        is_valid = (batch_index >= 0) & (batch_index < micro_count)
        slot_index = jnp.clip(batch_index, 0, micro_count - 1)
        own_input = lax.dynamic_index_in_dim(
            own_inputs, jnp.minimum(tick_index, micro_count - 1), 0, keepdims=False
        )
        layer_input = jnp.where(section_index == 0, own_input, received)
        output, kept = layer_forward(layer_input.astype(jnp.float32), weights, params)
        output_low = output.astype(jnp.bfloat16)
        passed = from_behind(output_low, "pipe", 1)
        outputs = store_slot(outputs, slot_index, is_valid, output_low)
        layer_inputs = store_slot(layer_inputs, slot_index, is_valid, layer_input)
        return ((passed, outputs, layer_inputs, buffers), None)

    tick_range = jnp.arange(micro_count + 1)
    forward_out, unused = lax.scan(
        forward_tick, (zero_rows, zero_stack, zero_stack, kept_buffers), tick_range
    )
    unused_rows, outputs, layer_inputs, kept_buffers = forward_out
    weight_acc = tuple((jnp.zeros(part.shape, jnp.float32) for part in weights))
    vector_acc = tuple((jnp.zeros(part.shape, jnp.float32) for part in params))
    grads_init = jnp.zeros((micro_count, row_count, feature_count), jnp.float32)
    live_rows = live_clips[:, 0]
    cot_rows_all = cotangent[:, 0]

    def backward_tick(state_carry, tick_index):
        received, grads_in, weight_sum, vector_sum = state_carry
        batch_index = micro_count - tick_index - section_index
        is_valid = (batch_index >= 0) & (batch_index < micro_count)
        slot_index = jnp.clip(batch_index, 0, micro_count - 1)
        cot_rows = lax.dynamic_index_in_dim(cot_rows_all, slot_index, 0, keepdims=False).astype(
            jnp.float32
        )
        live_flag = lax.dynamic_index_in_dim(live_rows, slot_index, 0, keepdims=False).astype(
            jnp.float32
        )
        grad_out = jnp.where(
            section_index == 1, cot_rows * live_flag, received.astype(jnp.float32)
        ) * is_valid.astype(jnp.float32)
        stored_input = lax.dynamic_index_in_dim(layer_inputs, slot_index, 0, keepdims=False)
        kept = layer_forward(stored_input.astype(jnp.float32), weights, params)[1]
        grad_in, weight_grads, vector_grads = layer_backward(grad_out, kept, weights, params)
        passed = from_behind(grad_in.astype(jnp.bfloat16), "pipe", -1)
        grads_in = store_slot(grads_in, slot_index, is_valid, grad_in)
        weight_sum = jax.tree.map(jnp.add, weight_sum, weight_grads)
        vector_sum = jax.tree.map(jnp.add, vector_sum, vector_grads)
        return ((passed, grads_in, weight_sum, vector_sum), None)

    backward_out, unused_two = lax.scan(
        backward_tick, (zero_rows, grads_init, weight_acc, vector_acc), tick_range
    )
    unused_grad, grads_in, weight_acc, vector_acc = backward_out
    weight_out = reduce_end(weight_acc)
    split_out = lax.psum((vector_acc[2], vector_acc[3], vector_acc[7]), "row")
    whole_out = lax.psum(
        (vector_acc[0], vector_acc[1], vector_acc[4], vector_acc[5], vector_acc[6], vector_acc[8]),
        ("row", "col"),
    )
    return (
        outputs[None, :, None],
        grads_in[None, :, None],
        whole_out[0][None],
        whole_out[1][None],
        weight_out[0][None],
        split_out[0][None],
        split_out[1][None],
        weight_out[1][None],
        whole_out[2][None],
        whole_out[3][None],
        whole_out[4][None],
        weight_out[2][None],
        split_out[2][None],
        weight_out[3][None],
        whole_out[5][None],
    )


def contract(left, right, left_dim, right_dim):
    return lax.dot_general(
        left, right, (((left_dim,), (right_dim,)), ((), ())), preferred_element_type=jnp.float32
    )


QUERY_BLOCK = 256


def attention_forward_kernel(q_ref, k_ref, v_ref, context_ref, lse_ref):
    frames = q_ref.shape[0]
    score_scale = 1.0 / math.sqrt(HD)
    for start in range(0, frames, QUERY_BLOCK):
        rows = slice(start, start + QUERY_BLOCK)
        parts = []
        for head in range(2):
            lanes = slice(head * HD, (head + 1) * HD)
            scaled = q_ref[rows, lanes] * jnp.asarray(score_scale, jnp.bfloat16)
            scores = contract(k_ref[:, lanes], scaled, 1, 1)
            top = jnp.max(scores, axis=0, keepdims=True)
            weights = jnp.exp(scores - top)
            total = jnp.sum(weights, axis=0, keepdims=True)
            mixed = contract(v_ref[:, lanes], weights.astype(jnp.bfloat16), 0, 0)
            parts.append(mixed / total)
            lse_ref[0, head : head + 1, rows] = top + jnp.log(total)
        pair = jnp.concatenate(parts, axis=0)
        context_ref[rows, :] = pair.T.astype(jnp.bfloat16)


def attention_forward(qkv):
    frames = qkv.shape[0]
    width = qkv.shape[1] // 3
    pairs = width // (2 * HD)

    def column(part):
        return pl.BlockSpec((frames, 2 * HD), lambda pair: (0, pair + part * pairs))

    return pl.pallas_call(
        attention_forward_kernel,
        grid=(pairs,),
        in_specs=[column(0), column(1), column(2)],
        out_specs=[
            pl.BlockSpec((frames, 2 * HD), lambda pair: (0, pair)),
            pl.BlockSpec((1, 8, frames), lambda pair: (pair, 0, 0)),
        ],
        out_shape=[
            jax.ShapeDtypeStruct((frames, width), jnp.bfloat16),
            jax.ShapeDtypeStruct((pairs, 8, frames), jnp.float32),
        ],
        compiler_params=pltpu.CompilerParams(vmem_limit_bytes=40 * 1024 * 1024),
        cost_estimate=pl.CostEstimate(
            flops=4 * frames * frames * width,
            bytes_accessed=8 * frames * width,
            transcendentals=frames * frames * width // HD,
        ),
        name="attention_forward",
    )(qkv, qkv, qkv)


def attention_backward_kernel(q_ref, k_ref, v_ref, grad_ref, lse_ref, out_ref, bias_ref):
    frames = q_ref.shape[0]
    width = out_ref.shape[1] // 3
    pair_index = pl.program_id(0)
    score_scale = 1.0 / math.sqrt(HD)
    grad_keys = [None, None]
    grad_values = [None, None]
    query_total = jnp.zeros((1, 2 * HD), jnp.float32)

    def columns(part):
        return pl.ds(pl.multiple_of(part * width + pair_index * (2 * HD), 2 * HD), 2 * HD)

    for start in range(0, frames, QUERY_BLOCK):
        rows = slice(start, start + QUERY_BLOCK)
        parts = []
        for head in range(2):
            lanes = slice(head * HD, (head + 1) * HD)
            keys = k_ref[:, lanes]
            grads = grad_ref[rows, lanes]
            scaled = q_ref[rows, lanes] * jnp.asarray(score_scale, jnp.bfloat16)
            scores = contract(keys, scaled, 1, 1)
            probs = jnp.exp(scores - lse_ref[0, head : head + 1, rows])
            grad_probs = contract(v_ref[:, lanes], grads, 1, 1)
            delta = jnp.sum(probs * grad_probs, axis=0, keepdims=True)
            low_scores = (probs * (grad_probs - delta)).astype(jnp.bfloat16)
            value_part = contract(probs.astype(jnp.bfloat16), grads, 1, 0)
            key_part = contract(low_scores, scaled, 1, 0)
            grad_values[head] = value_part if start == 0 else grad_values[head] + value_part
            grad_keys[head] = key_part if start == 0 else grad_keys[head] + key_part
            parts.append(contract(keys, low_scores, 0, 0))
        pair = jnp.concatenate(parts, axis=0).T * score_scale
        query_total = query_total + jnp.sum(pair, axis=0, keepdims=True)
        out_ref[rows, columns(0)] = pair.astype(jnp.bfloat16)
    key_pair = jnp.concatenate(grad_keys, axis=1)
    value_pair = jnp.concatenate(grad_values, axis=1)
    out_ref[:, columns(1)] = key_pair.astype(jnp.bfloat16)
    out_ref[:, columns(2)] = value_pair.astype(jnp.bfloat16)
    bias_ref[0:1, columns(0)] = query_total
    bias_ref[0:1, columns(2)] = jnp.sum(value_pair, axis=0, keepdims=True)


def attention_backward(qkv, grad_context, lse):
    frames = qkv.shape[0]
    width = qkv.shape[1] // 3
    pairs = width // (2 * HD)

    def column(part):
        return pl.BlockSpec((frames, 2 * HD), lambda pair: (0, pair + part * pairs))

    return pl.pallas_call(
        attention_backward_kernel,
        grid=(pairs,),
        in_specs=[
            column(0),
            column(1),
            column(2),
            column(0),
            pl.BlockSpec((1, 8, frames), lambda pair: (pair, 0, 0)),
        ],
        out_specs=[
            pl.BlockSpec((frames, 3 * width), lambda pair: (0, 0)),
            pl.BlockSpec((8, 3 * width), lambda pair: (0, 0)),
        ],
        out_shape=[
            jax.ShapeDtypeStruct((frames, 3 * width), jnp.bfloat16),
            jax.ShapeDtypeStruct((8, 3 * width), jnp.float32),
        ],
        compiler_params=pltpu.CompilerParams(vmem_limit_bytes=40 * 1024 * 1024),
        cost_estimate=pl.CostEstimate(
            flops=10 * frames * frames * width,
            bytes_accessed=14 * frames * width,
            transcendentals=frames * frames * width // HD,
        ),
        name="attention_backward",
    )(qkv, qkv, qkv, grad_context, lse)


def cut_block(block, width, hidden):
    edge = 4 * width
    return (
        block[:, : 3 * width],
        block[:, 3 * width : edge],
        block[:, edge : edge + hidden],
        block[:, edge + hidden :],
    )


def clip_forward(values, blocks, params):
    (
        gain_one,
        shift_one,
        qkv_bias,
        proj_bias,
        gain_two,
        shift_two,
        up_bias,
        down_bias,
    ) = params
    centered_one, inv_one, normed_one = norm_forward(values, gain_one, shift_one)
    qkv_parts, contexts, lses, pre_acts, activated = [], [], [], [], []
    attended = proj_bias
    for (qkv_full, proj_turned, up_full, down_turned), bias in zip(blocks, qkv_bias):
        qkv = (contract(normed_one, qkv_full, 1, 0) + bias).astype(jnp.bfloat16)
        context, lse = attention_forward(qkv)
        attended = attended + contract(context, proj_turned, 1, 1)
        qkv_parts.append(qkv)
        contexts.append(context)
        lses.append(lse)
    hidden = values + attended
    centered_two, inv_two, normed_two = norm_forward(hidden, gain_two, shift_two)
    output = hidden + down_bias
    for (qkv_full, proj_turned, up_full, down_turned), bias in zip(blocks, up_bias):
        pre_act = contract(normed_two, up_full, 1, 0) + bias
        active = exact_gelu(pre_act).astype(jnp.bfloat16)
        output = output + contract(active, down_turned, 1, 1)
        pre_acts.append(pre_act)
        activated.append(active)
    kept = (
        centered_one,
        inv_one,
        normed_one,
        qkv_parts,
        contexts,
        lses,
        centered_two,
        inv_two,
        normed_two,
        pre_acts,
        activated,
    )
    return (output, kept)


def clip_backward(grad_out, kept, blocks, params):
    gain_one, gain_two = (params[0], params[4])
    (
        centered_one,
        inv_one,
        normed_one,
        qkv_parts,
        contexts,
        lses,
        centered_two,
        inv_two,
        normed_two,
        pre_acts,
        activated,
    ) = kept
    grad_down_bias = jnp.sum(grad_out, axis=0)
    down_grad = grad_out.astype(jnp.bfloat16)
    grad_normed_two = 0.0
    up_biases, early, late, query_biases, value_biases = [], [], [], [], []
    for (qkv_full, proj_turned, up_full, down_turned), pre_act, active in zip(
        blocks, pre_acts, activated
    ):
        grad_down = contract(down_grad, active, 0, 0)
        grad_act = contract(down_grad, down_turned, 1, 0)
        grad_pre = jax.vjp(exact_gelu, pre_act)[1](grad_act)[0]
        up_biases.append(jnp.sum(grad_pre, axis=0))
        grad_pre_low = grad_pre.astype(jnp.bfloat16)
        grad_up = contract(normed_two, grad_pre_low, 0, 0)
        grad_normed_two = grad_normed_two + contract(grad_pre_low, up_full, 1, 1)
        early.append((grad_up.astype(jnp.bfloat16), grad_down.astype(jnp.bfloat16)))
    grad_hidden_norm, grad_gain_two, grad_shift_two = norm_backward(
        grad_normed_two, centered_two, inv_two, gain_two
    )
    grad_hidden = grad_out + grad_hidden_norm
    grad_proj_bias = jnp.sum(grad_hidden, axis=0)
    proj_grad = grad_hidden.astype(jnp.bfloat16)
    grad_normed_one = 0.0
    for (qkv_full, proj_turned, up_full, down_turned), qkv, context, lse in zip(
        blocks, qkv_parts, contexts, lses
    ):
        width = context.shape[1]
        grad_proj = contract(proj_grad, context, 0, 0)
        grad_context = contract(proj_grad, proj_turned, 1, 0).astype(jnp.bfloat16)
        grad_qkv_low, bias_rows = attention_backward(qkv, grad_context, lse)
        query_biases.append(bias_rows[0, :width])
        value_biases.append(bias_rows[0, 2 * width :])
        grad_qkv = contract(normed_one, grad_qkv_low, 0, 0)
        grad_normed_one = grad_normed_one + contract(grad_qkv_low, qkv_full, 1, 1)
        late.append((grad_qkv.astype(jnp.bfloat16), grad_proj.astype(jnp.bfloat16)))
    grad_in_norm, grad_gain_one, grad_shift_one = norm_backward(
        grad_normed_one, centered_one, inv_one, gain_one
    )
    grad_in = grad_hidden + grad_in_norm
    whole = jnp.concatenate(
        [
            grad_gain_one,
            grad_shift_one,
            grad_proj_bias,
            grad_gain_two,
            grad_shift_two,
            grad_down_bias,
        ]
    )
    split = jnp.stack(
        [jnp.concatenate(part) for part in zip(query_biases, value_biases, up_biases)]
    )
    return (grad_in, early, late, whole, split)


GROUP = ("pipe", "col")
EVERY = ("pipe", "col", "row")


def trade(pieces, place, targets):
    count = len(pieces)
    stacked = jnp.stack(pieces)
    taken = [lax.dynamic_index_in_dim(stacked, place, 0, keepdims=False)]
    for step in range(1, count):
        sent = lax.dynamic_index_in_dim(stacked, place ^ step, 0, keepdims=False)
        taken.append(
            lax.ppermute(
                sent,
                GROUP,
                [(here, here ^ step) for here in range(count) if here ^ step in targets],
            )
        )
    return taken


def in_order(taken, place):
    stacked = jnp.stack(taken)
    return jnp.stack(
        [
            lax.dynamic_index_in_dim(stacked, place ^ index, 0, keepdims=False)
            for index in range(len(taken))
        ]
    )


def swap_columns(own, other, col):
    got = lax.ppermute(other, "col", [(0, 1), (1, 0)])
    return jnp.where(
        col == 0, jnp.concatenate([own, got]), jnp.concatenate([got, own])
    )


def gather_blocks(block):
    full = lax.all_gather(block, EVERY, axis=0, tiled=True)
    return full.reshape(lax.axis_size(GROUP), -1, block.shape[1])


def on_device_clip(
    inputs,
    first_gain,
    first_shift,
    qkv_weight,
    query_bias,
    value_bias,
    proj_weight,
    proj_bias,
    second_gain,
    second_shift,
    up_weight,
    up_bias,
    down_weight,
    down_bias,
    cotangent,
    live_clips,
):
    section, col = (lax.axis_index("pipe"), lax.axis_index("col"))
    place = 2 * section + col
    width, hidden_width = (qkv_weight.shape[3], up_weight.shape[2])
    features = inputs.shape[3]
    half = inputs.shape[2]
    early_block = jnp.concatenate(
        [qkv_weight[0, 0], qkv_weight[0, 1], qkv_weight[0, 2], proj_weight[0].T], axis=1
    )
    late_block = jnp.concatenate([up_weight[0], down_weight[0].T], axis=1)
    early_full = gather_blocks(early_block)
    late_full = gather_blocks(late_block)
    vectors = lax.all_gather(
        jnp.concatenate(
            [
                first_gain[0],
                first_shift[0],
                proj_bias[0],
                second_gain[0],
                second_shift[0],
                down_bias[0],
                query_bias[0],
                value_bias[0],
                up_bias[0],
            ]
        ),
        GROUP,
        axis=0,
        tiled=False,
    )
    blocks, params = ([], [])
    for layer in range(2):
        blocks.append(
            [
                (
                    early_full[2 * layer + part][:, : 3 * width],
                    early_full[2 * layer + part][:, 3 * width :],
                    late_full[2 * layer + part][:, :hidden_width],
                    late_full[2 * layer + part][:, hidden_width:],
                )
                for part in range(2)
            ]
        )
        rows = vectors[2 * layer]
        whole = [rows[index * features : (index + 1) * features] for index in range(6)]
        tails = [vectors[2 * layer + part][6 * features :] for part in range(2)]
        params.append(
            (
                whole[0],
                whole[1],
                [
                    jnp.concatenate(
                        [tail[:width], jnp.zeros((width,), jnp.float32), tail[width : 2 * width]]
                    )
                    for tail in tails
                ],
                whole[2],
                whole[3],
                whole[4],
                [tail[2 * width :] for tail in tails],
                whole[5],
            )
        )

    def own_clip(rows):
        own = lax.dynamic_index_in_dim(rows[:, 0], place, 0, keepdims=False)
        other = lax.dynamic_index_in_dim(rows[:, 0], place ^ 1, 0, keepdims=False)
        return swap_columns(own, other, col)

    values = own_clip(inputs).astype(jnp.float32)
    live_flag = lax.dynamic_index_in_dim(live_clips[:, 0], place, 0, keepdims=False)
    grad_final = own_clip(cotangent).astype(jnp.float32) * live_flag.astype(jnp.float32)
    first, kept_first = clip_forward(values, blocks[0], params[0])
    sent = first.astype(jnp.bfloat16)
    second, kept_second = clip_forward(sent.astype(jnp.float32), blocks[1], params[1])
    final = second.astype(jnp.bfloat16)
    states = in_order(
        trade([sent[:half], sent[half:], final[:half], final[half:]], place, (0, 1, 2, 3)), place
    )

    def reduce_grads(early, late):
        quarter = hidden_width // 2
        first_half = [
            jnp.concatenate([part[0], part[1], up_part[0][:, :quarter]], axis=1)
            for part, up_part in zip(late, early)
        ]
        second_half = [
            jnp.concatenate([up_part[0][:, quarter:], up_part[1]], axis=1) for up_part in early
        ]
        stacked = jnp.concatenate(first_half + second_half, axis=0)
        return lax.psum_scatter(stacked, EVERY, scatter_dimension=0, tiled=True)

    grad_mid, early, late, whole_second, split_second = clip_backward(
        grad_final, kept_second, blocks[1], params[1]
    )
    mid_low = grad_mid.astype(jnp.bfloat16)
    own_second = reduce_grads(early, late)
    mid_taken = trade([mid_low[:half], mid_low[half:]] * 2, place, (2, 3))
    grad_start, early, late, whole_first, split_first = clip_backward(
        mid_low.astype(jnp.float32), kept_first, blocks[0], params[0]
    )
    own_first = reduce_grads(early, late)
    start_low = grad_start.astype(jnp.bfloat16)
    start_taken = trade([start_low[:half], start_low[half:]] * 2, place, (0, 1))
    grads_in = in_order(
        [jnp.where(section == 1, mid, start) for mid, start in zip(mid_taken, start_taken)], place
    ).astype(jnp.float32)
    kept_half = jnp.where(section == 0, own_first, own_second)
    moved = lax.ppermute(
        jnp.where(section == 0, own_second, own_first), "pipe", [(0, 1), (1, 0)]
    )
    packed = jnp.where(
        section == 0,
        jnp.concatenate([kept_half, moved], axis=1),
        jnp.concatenate([moved, kept_half], axis=1),
    ).astype(jnp.float32)
    grad_qkv, grad_proj, grad_up, grad_down = cut_block(packed, width, hidden_width)
    whole_all, split_all = lax.psum(
        (jnp.stack([whole_first, whole_second]), jnp.stack([split_first, split_second])), EVERY
    )
    whole_out = lax.dynamic_index_in_dim(whole_all, section, 0, keepdims=False).reshape(
        6, 1, features
    )
    split_out = lax.dynamic_index_in_dim(split_all, section, 0, keepdims=False)
    split_out = lax.dynamic_index_in_dim(split_out, col, 0, keepdims=False)
    return (
        states[None, :, None],
        grads_in[None, :, None],
        whole_out[0],
        whole_out[1],
        jnp.stack([grad_qkv[:, part * width : (part + 1) * width] for part in range(3)])[None],
        split_out[None, :width],
        split_out[None, width : 2 * width],
        grad_proj.T[None],
        whole_out[2],
        whole_out[3],
        whole_out[4],
        grad_up[None],
        split_out[None, 2 * width :],
        grad_down.T[None],
        whole_out[5],
    )


def one_clip_each(mesh):
    sizes = dict(mesh.shape)
    return sizes["pipe"] == 2 and sizes["col"] == 2


def choose(mesh):
    def body(*arrays):
        fits = one_clip_each(mesh) and arrays[0].shape[:2] == (4, 1)
        return (on_device_clip if fits else on_device)(*arrays)

    return body


def solution(mesh):
    placed = (
        P(None, "row", "col", None),
        P("pipe", None),
        P("pipe", None),
        P("pipe", None, "row", "col"),
        P("pipe", "col"),
        P("pipe", "col"),
        P("pipe", "col", "row"),
        P("pipe", None),
        P("pipe", None),
        P("pipe", None),
        P("pipe", "row", "col"),
        P("pipe", "col"),
        P("pipe", "col", "row"),
        P("pipe", None),
        P(None, "row", "col", None),
        P(None, "row"),
    )
    return jax.shard_map(
        choose(mesh),
        mesh=mesh,
        in_specs=placed,
        out_specs=(
            P("pipe", None, "row", "col", None),
            P("pipe", None, "row", "col", None),
            P("pipe", None),
            P("pipe", None),
            P("pipe", None, "row", "col"),
            P("pipe", "col"),
            P("pipe", "col"),
            P("pipe", "col", "row"),
            P("pipe", None),
            P("pipe", None),
            P("pipe", None),
            P("pipe", "row", "col"),
            P("pipe", "col"),
            P("pipe", "col", "row"),
            P("pipe", None),
        ),
        check_vma=False,
    )
```

profile of v0, /device:TPU:0, one launch (start us, length us, event | category | flops | bytes accessed | tf_op | source)
XLA Modules:
  0.0 613.1 jit_solution(4471829497163923032)
XLA Ops:
  12.9 3.0 collective-permute-start
  18.7 25.4 %all-gather.1 = f32[4,1,4608]{2,1,0:T(1,128)S(1)} all-gather(f32[1,1,4608]{2,1,0:T(1,128)S(1)} %reshape.265), channel_id=2, replica_groups=mesh['pipe'=2,'row'=8,'col'=2] {'pipe','col'}, dimensions={0}, use_global_device_ids=true | all-gather | bytes 92160 | tf_op jit(solution)/shard_map/all_gather | solution.py:714
  47.2 29.7 %all-gather.5.cloned.1.call-done = bf16[2048,1024]{1,0:T(8,128)(2,1)} async-done(((bf16[64,1024]{1,0:T(8,128)(2,1)}), bf16[2048,1024]{1,0:T(8,128)(2,1)}) %all-gather.5.cloned.1.call-update) | async-done | bytes 4194320 | tf_op jit(solution)/shard_map/all_gather | solution.py:681
  76.9 2.3 add_convert_fusion.3.q_ref.k_ref.v_ref
  79.2 12.5 %attention_forward.4 = (bf16[1024,256]{1,0:T(8,128)(2,1)S(1)}, f32[2,8,1024]{2,1,0:T(8,128)S(1)}) custom-call(bf16[1024,768]{1,0:T(8,128)(2,1)S(1)} %add_convert_fusion.3.q_ref.k_ref.v_ref, bf16[1024,768]{1,0:T(8,128)(2,1)S(1)} %add_convert_fusion.3.q_ref.k_ref.v_ref, bf16[1024,768]{1,0:T(8,128)(2,1)S(1)} %add_convert_fusion.3.q_ref.k_ref.v_ref), custom_call_target="tpu_custom_call" | custom-call | flops 1073741824 | bytes 2097152 | tf_op jit(solution)/shard_map/attention_forward/pallas_call | solution.py:419
  91.8 2.4 add_convert_fusion.2.q_ref.k_ref.v_ref
  94.2 12.6 %attention_forward.5 = (bf16[1024,256]{1,0:T(8,128)(2,1)S(1)}, f32[2,8,1024]{2,1,0:T(8,128)S(1)}) custom-call(bf16[1024,768]{1,0:T(8,128)(2,1)S(1)} %add_convert_fusion.2.q_ref.k_ref.v_ref, bf16[1024,768]{1,0:T(8,128)(2,1)S(1)} %add_convert_fusion.2.q_ref.k_ref.v_ref, bf16[1024,768]{1,0:T(8,128)(2,1)S(1)} %add_convert_fusion.2.q_ref.k_ref.v_ref), custom_call_target="tpu_custom_call" | custom-call | flops 1073741824 | bytes 2097152 | tf_op jit(solution)/shard_map/attention_forward/pallas_call | solution.py:419
  110.8 45.5 %all-gather.7.cloned.1.call-done = bf16[2048,2048]{1,0:T(8,128)(2,1)} async-done(((bf16[64,2048]{1,0:T(8,128)(2,1)}), bf16[2048,2048]{1,0:T(8,128)(2,1)}) %all-gather.7.cloned.1.call-update) | async-done | bytes 8388624 | tf_op jit(solution)/shard_map/all_gather | solution.py:681
  156.3 13.2 %multiply_convert_fusion.3 = (bf16[1024,1024]{1,0:T(8,128)(2,1)S(1)}, f32[1024,1024]{1,0:T(8,128)}, f32[1024,1024]{1,0:T(8,128)}) fusion(f32[1024]{0:T(1024)S(1)} %bitcast.260, bf16[1024,512]{0,1:T(8,128)(2,1)S(1)} %add_convert_fusion.7, bf16[2048,2048]{1,0:T(8,128)(2,1)} %all-gather.7.cloned.1.call-done), kind=kOutput, calls=%fused_computation.53 | convolution fusion | flops 1142947840 | bytes 12587008 | tf_op jit(solution)/shard_map/dot_general | solution.py:383
  170.8 11.7 %multiply_convert_fusion.2 = (bf16[1024,1024]{1,0:T(8,128)(2,1)S(1)}, f32[1024,1024]{1,0:T(8,128)}, f32[1024,1024]{1,0:T(8,128)}) fusion(f32[1024]{0:T(1024)S(1)} %bitcast.258, bf16[1024,512]{0,1:T(8,128)(2,1)S(1)} %add_convert_fusion.7, bf16[2048,2048]{1,0:T(8,128)(2,1)S(1)} %copy-done.59), kind=kOutput, calls=%fused_computation.40 | convolution fusion | flops 1142947840 | bytes 12587008 | tf_op jit(solution)/shard_map/dot_general | solution.py:383
  187.1 12.4 %attention_forward.6 = (bf16[1024,256]{1,0:T(8,128)(2,1)S(1)}, f32[2,8,1024]{2,1,0:T(8,128)S(1)}) custom-call(bf16[1024,768]{1,0:T(8,128)(2,1)S(1)} %add_convert_fusion.1.q_ref.k_ref.v_ref, bf16[1024,768]{1,0:T(8,128)(2,1)S(1)} %add_convert_fusion.1.q_ref.k_ref.v_ref, bf16[1024,768]{1,0:T(8,128)(2,1)S(1)} %add_convert_fusion.1.q_ref.k_ref.v_ref), custom_call_target="tpu_custom_call" | custom-call | flops 1073741824 | bytes 2097152 | tf_op jit(solution)/shard_map/attention_forward/pallas_call | solution.py:419
  200.7 12.5 %attention_forward.7 = (bf16[1024,256]{1,0:T(8,128)(2,1)S(1)}, f32[2,8,1024]{2,1,0:T(8,128)S(1)}) custom-call(bf16[1024,768]{1,0:T(8,128)(2,1)S(1)} %add_convert_fusion.q_ref.k_ref.v_ref, bf16[1024,768]{1,0:T(8,128)(2,1)S(1)} %add_convert_fusion.q_ref.k_ref.v_ref, bf16[1024,768]{1,0:T(8,128)(2,1)S(1)} %add_convert_fusion.q_ref.k_ref.v_ref), custom_call_target="tpu_custom_call" | custom-call | flops 1073741824 | bytes 2097152 | tf_op jit(solution)/shard_map/attention_forward/pallas_call | solution.py:419
  215.0 26.7 %multiply_convert_fusion = (bf16[1024,1024]{1,0:T(8,128)(2,1)}, f32[1024,1024]{1,0:T(8,128)S(1)}, f32[1024,1024]{1,0:T(8,128)}) fusion(f32[1024]{0:T(1024)S(1)} %bitcast.264, bf16[1024,512]{0,1:T(8,128)(2,1)S(1)} %add_convert_fusion.5, bf16[2048,2048]{1,0:T(8,128)(2,1)S(1)} %copy-done.59), kind=kOutput, calls=%fused_computation.14 | convolution fusion | flops 1142947840 | bytes 12587008 | tf_op jit(solution)/shard_map/dot_general | solution.py:383
  241.7 6.3 %fusion.148 = (f32[1024]{0:T(1024)S(1)}, bf16[1024,1024]{1,0:T(8,128)(2,1)S(1)}) fusion(f32[1024,1024]{1,0:T(8,128)S(1)} %get-tuple-element.117, bf16[2048,2048]{1,0:T(8,128)(2,1)S(1)} %copy-done.59, f32[]{:T(128)} %bitcast.56, bf16[512,512]{0,1:T(8,128)(2,1)S(1)} %bitcast.206, bf16[512,512]{0,1:T(8,128)(2,1)} %collective-permute-done.4, pred[]{:T(512)S(6)} %eq.6, ...), kind=kOutput, calls=%fused_computation.344 | convolution fusion | flops 1096809472 | bytes 12591109 | tf_op jit(solution)/shard_map/dot_general | solution.py:383
  249.4 11.5 %multiply_convert_fusion.1 = (bf16[1024,1024]{1,0:T(8,128)(2,1)}, f32[1024,1024]{1,0:T(8,128)}, f32[1024,1024]{1,0:T(8,128)}) fusion(f32[1024]{0:T(1024)S(1)} %bitcast.262, bf16[1024,512]{0,1:T(8,128)(2,1)S(1)} %add_convert_fusion.5, bf16[2048,2048]{1,0:T(8,128)(2,1)S(1)} %copy-done.59), kind=kOutput, calls=%fused_computation.27 | convolution fusion | flops 1142947840 | bytes 12587008 | tf_op jit(solution)/shard_map/dot_general | solution.py:383
  260.9 7.4 %fusion.149 = (f32[1024]{0:T(1024)S(1)}, bf16[1024,1024]{1,0:T(8,128)(2,1)S(1)}) fusion(f32[1024,1024]{1,0:T(8,128)} %get-tuple-element.119, bf16[2048,2048]{1,0:T(8,128)(2,1)S(1)} %copy-done.59, f32[]{:T(128)} %bitcast.56, bf16[512,512]{0,1:T(8,128)(2,1)S(1)} %bitcast.207, bf16[512,512]{0,1:T(8,128)(2,1)} %collective-permute-done.4, pred[]{:T(512)S(6)} %eq.6, ...), kind=kOutput, calls=%fused_computation.345 | convolution fusion | flops 1096809472 | bytes 12591109 | tf_op jit(solution)/shard_map/dot_general | solution.py:383
  270.9 2.0 multiply_reduce_fusion
  272.9 3.2 fusion.128
  277.6 15.2 %attention_backward.4 = (bf16[1024,768]{1,0:T(8,128)(2,1)S(1)}, f32[8,768]{1,0:T(8,128)S(1)}) custom-call(bf16[1024,768]{1,0:T(8,128)(2,1)S(1)} %add_convert_fusion.1.q_ref.k_ref.v_ref, bf16[1024,768]{1,0:T(8,128)(2,1)S(1)} %add_convert_fusion.1.q_ref.k_ref.v_ref, bf16[1024,768]{1,0:T(8,128)(2,1)S(1)} %add_convert_fusion.1.q_ref.k_ref.v_ref, ...), custom_call_target="tpu_custom_call" | custom-call | flops 2684354560 | bytes 3670016 | tf_op jit(solution)/shard_map/attention_backward/pallas_call | solution.py:490
  294.5 15.0 %attention_backward.5 = (bf16[1024,768]{1,0:T(8,128)(2,1)S(1)}, f32[8,768]{1,0:T(8,128)S(1)}) custom-call(bf16[1024,768]{1,0:T(8,128)(2,1)S(1)} %add_convert_fusion.q_ref.k_ref.v_ref, bf16[1024,768]{1,0:T(8,128)(2,1)S(1)} %add_convert_fusion.q_ref.k_ref.v_ref, bf16[1024,768]{1,0:T(8,128)(2,1)S(1)} %add_convert_fusion.q_ref.k_ref.v_ref, ...), custom_call_target="tpu_custom_call" | custom-call | flops 2684354560 | bytes 3670016 | tf_op jit(solution)/shard_map/attention_backward/pallas_call | solution.py:490
  311.1 3.3 convolution_convert_fusion
  314.4 3.1 convolution_convert_fusion.1
  317.5 29.7 %maximum_maximum_fusion.1 = bf16[2048,1536]{1,0:T(8,128)(2,1)} fusion(bf16[512,1024]{1,0:T(8,128)(2,1)S(1)} %convolution_convert_fusion, bf16[512,512]{1,0:T(8,128)(2,1)S(1)} %get-tuple-element.243, bf16[512,1024]{1,0:T(8,128)(2,1)S(1)} %convolution_convert_fusion.1, bf16[512,512]{1,0:T(8,128)(2,1)S(1)} %get-tuple-element.152, ...), kind=kLoop, calls=%fused_computation.1 | loop fusion | flops 62914560 | bytes 12582912 | tf_op jit(solution)/shard_map/concatenate | solution.py:791
  347.3 2.3 fusion.90
  349.6 2.9 fusion.43
  355.7 3.2 fusion.151
  362.7 3.1 fusion.150
  365.8 1.9 multiply_reduce_fusion.1
  368.8 2.3 convolution_convert_fusion.13.grad_ref
  371.2 15.3 %attention_backward.6 = (bf16[1024,768]{1,0:T(8,128)(2,1)S(1)}, f32[8,768]{1,0:T(8,128)S(1)}) custom-call(bf16[1024,768]{1,0:T(8,128)(2,1)S(1)} %copy-done.7, bf16[1024,768]{1,0:T(8,128)(2,1)S(1)} %copy-done.7, bf16[1024,768]{1,0:T(8,128)(2,1)S(1)} %copy-done.7, bf16[1024,256]{1,0:T(8,128)(2,1)S(1)} %convolution_convert_fusion.13.grad_ref, ...), custom_call_target="tpu_custom_call" | custom-call | flops 2684354560 | bytes 3670016 | tf_op jit(solution)/shard_map/attention_backward/pallas_call | solution.py:490
  388.0 15.2 %attention_backward.7 = (bf16[1024,768]{1,0:T(8,128)(2,1)S(1)}, f32[8,768]{1,0:T(8,128)S(1)}) custom-call(bf16[1024,768]{1,0:T(8,128)(2,1)S(1)} %copy-done.5, bf16[1024,768]{1,0:T(8,128)(2,1)S(1)} %copy-done.5, bf16[1024,768]{1,0:T(8,128)(2,1)S(1)} %copy-done.5, bf16[1024,256]{1,0:T(8,128)(2,1)S(1)} %convolution_convert_fusion.12.grad_ref, ...), custom_call_target="tpu_custom_call" | custom-call | flops 2684354560 | bytes 3670016 | tf_op jit(solution)/shard_map/attention_backward/pallas_call | solution.py:490
  413.7 29.6 %maximum_maximum_fusion = bf16[2048,1536]{1,0:T(8,128)(2,1)} fusion(bf16[512,1024]{1,0:T(8,128)(2,1)S(1)} %convolution_convert_fusion.4, bf16[512,512]{1,0:T(8,128)(2,1)S(1)} %get-tuple-element.150, bf16[512,1024]{1,0:T(8,128)(2,1)S(1)} %convolution_convert_fusion.5, bf16[512,512]{1,0:T(8,128)(2,1)S(1)} %get-tuple-element.148, ...), kind=kLoop, calls=%fused_computation | loop fusion | flops 62914560 | bytes 12582912 | tf_op jit(solution)/shard_map/concatenate | solution.py:791
  443.4 2.3 fusion.95
  446.1 3.1 fusion.52
  453.4 3.3 collective-permute-start.6
  456.8 3.2 collective-permute-start.7
  461.5 46.8 %all-reduce = (f32[2,3072]{1,0:T(2,128)S(1)}, f32[2,2,1536]{2,1,0:T(2,128)S(1)}) all-reduce(f32[2,3072]{1,0:T(2,128)S(1)} %pad_maximum_fusion.7, f32[2,2,1536]{2,1,0:T(2,128)S(1)} %pad_maximum_fusion.8), channel_id=1, replica_groups=mesh['pipe'=2,'row'=8,'col'=2] {'pipe','col','row'}, use_global_device_ids=true, to_apply=%region_28.29 | all-reduce | flops 12288 | bytes 98304 | tf_op jit(solution)/shard_map/psum | solution.py:819
  509.1 3.3 fusion.72
  512.4 2.5 add_convert_fusion.4
  519.3 5.5 collective-permute-start.9
  524.8 2.3 collective-permute-start.1
  530.9 11.2 %collective-permute-done.10 = bf16[512,512]{0,1:T(8,128)(2,1)S(1)} collective-permute-done((bf16[512,512]{0,1:T(8,128)(2,1)S(1)}, bf16[512,512]{0,1:T(8,128)(2,1)S(1)}, u32[]{:S(2)}, u32[]{:S(2)}) %collective-permute-start.10) | collective-permute-done | bytes 524320 | tf_op jit(solution)/shard_map/ppermute | solution.py:654
  545.1 6.8 %collective-permute-done.1 = bf16[512,512]{0,1:T(8,128)(2,1)} collective-permute-done((bf16[512,512]{0,1:T(8,128)(2,1)}, bf16[512,512]{0,1:T(8,128)(2,1)}, u32[]{:S(2)}, u32[]{:S(2)}) %collective-permute-start.1) | collective-permute-done | bytes 524320 | tf_op jit(solution)/shard_map/ppermute | solution.py:654
  552.8 11.2 %collective-permute-done.3 = bf16[512,512]{0,1:T(8,128)(2,1)} collective-permute-done((bf16[512,512]{0,1:T(8,128)(2,1)}, bf16[512,512]{0,1:T(8,128)(2,1)}, u32[]{:S(2)}, u32[]{:S(2)}) %collective-permute-start.3) | collective-permute-done | bytes 524320 | tf_op jit(solution)/shard_map/ppermute | solution.py:654
  564.0 1.8 pad_maximum_fusion.1
  566.2 2.4 copy.101
  568.6 28.6 %reduce-scatter.3.cloned.1.call-done = bf16[64,1536]{1,0:T(8,128)(2,1)} async-done(((bf16[2048,1536]{1,0:T(8,128)(2,1)}), bf16[64,1536]{1,0:T(8,128)(2,1)}) %reduce-scatter.3.cloned.1.call-update) | async-done | bytes 196624 | tf_op jit(solution)/shard_map/reduce_scatter | solution.py:792
  599.8 3.6 maximum_convert_fusion
  (316 shorter events, 76.6 us)
Async XLA Ops:
  7.2 69.7 %all-gather.5.cloned.1.call-start = ((), (), s32[]{:S(2)}) async-start(), calls=%async_computation.2 | async-start | bytes 4325376 | tf_op jit(solution)/shard_map/all_gather | solution.py:681
  9.5 9.1 %copy-start.53 = (f32[1,512]{1,0:T(1,128)S(1)}, f32[1,512]{1,0:T(1,128)}, u32[]{:S(2)}) copy-start(f32[1,512]{1,0:T(1,128)} %param.23) | copy-start | bytes 6148
  9.5 9.1 %copy-start.54 = (f32[1,512]{1,0:T(1,128)S(1)}, f32[1,512]{1,0:T(1,128)}, u32[]{:S(2)}) copy-start(f32[1,512]{1,0:T(1,128)} %param.24) | copy-start | bytes 6148
  9.5 9.1 %copy-start.55 = (f32[1,512]{1,0:T(1,128)S(1)}, f32[1,512]{1,0:T(1,128)}, u32[]{:S(2)}) copy-start(f32[1,512]{1,0:T(1,128)} %param.25) | copy-start | bytes 6148
  9.5 9.1 %copy-start.56 = (f32[1,512]{1,0:T(1,128)S(1)}, f32[1,512]{1,0:T(1,128)}, u32[]{:S(2)}) copy-start(f32[1,512]{1,0:T(1,128)} %param.29) | copy-start | bytes 6148
  9.5 9.1 %copy-start.57 = (f32[1,256]{1,0:T(1,128)S(1)}, f32[1,256]{1,0:T(1,128)}, u32[]{:S(2)}) copy-start(f32[1,256]{1,0:T(1,128)} %param.20) | copy-start | bytes 3076
  9.5 9.1 %copy-start.58 = (f32[1,256]{1,0:T(1,128)S(1)}, f32[1,256]{1,0:T(1,128)}, u32[]{:S(2)}) copy-start(f32[1,256]{1,0:T(1,128)} %param.21) | copy-start | bytes 3076
  9.5 9.1 %copy-start.45 = (f32[1,1024]{1,0:T(1,128)S(1)}, f32[1,1024]{1,0:T(1,128)}, u32[]{:S(2)}) copy-start(f32[1,1024]{1,0:T(1,128)} %param.27) | copy-start | bytes 12292
  9.5 146.8 %all-gather.7.cloned.1.call-start = ((), (), s32[]{:S(2)}) async-start(), calls=%async_computation.3 | async-start | bytes 8650752 | tf_op jit(solution)/shard_map/all_gather | solution.py:681
  11.3 557.3 %reduce-scatter.5.cloned.1.call-start = ((), (), s32[]{:S(2)}) async-start(), calls=%async_computation.5 | async-start | bytes 6488064 | tf_op jit(solution)/shard_map/reduce_scatter | solution.py:792
  11.4 33.7 %copy-start.60 = (s32[4,1]{0,1:T(1,128)S(1)}, s32[4,1]{0,1:T(1,128)}, u32[]{:S(2)}) copy-start(s32[4,1]{0,1:T(1,128)} %param.31) | copy-start | bytes 52
  12.9 33.5 %collective-permute-start = (bf16[512,512]{0,1:T(8,128)(2,1)S(1)}, bf16[512,512]{0,1:T(8,128)(2,1)S(1)}, u32[]{:S(2)}, u32[]{:S(2)}) collective-permute-start(bf16[512,512]{0,1:T(8,128)(2,1)S(1)} %bitcast.211), channel_id=1, source_target_pairs={{0,1},{1,0},{2,3},{3,2},{4,5},{5,4},{6,7},{7,6},{8,9},{9,8},{10,11... | collective-permute-start | bytes 1572872 | tf_op jit(solution)/shard_map/ppermute | solution.py:674
  18.2 223.5 %collective-permute-start.4 = (bf16[512,512]{0,1:T(8,128)(2,1)}, bf16[512,512]{0,1:T(8,128)(2,1)}, u32[]{:S(2)}, u32[]{:S(2)}) collective-permute-start(bf16[512,512]{0,1:T(8,128)(2,1)} %bitcast.55), channel_id=1, source_target_pairs={{0,1},{1,0},{2,3},{3,2},{4,5},{5,4},{6,7},{7,6},{8,9},{9,8},{10,11... | collective-permute-start | bytes 1572872 | tf_op jit(solution)/shard_map/ppermute | solution.py:674
  18.5 90.0 %copy-start.19 = (bf16[1,1,512,512]{2,3,1,0:T(8,128)(2,1)}, bf16[1,1,512,512]{2,3,1,0:T(8,128)(2,1)S(1)}, u32[]{:S(2)}) copy-start(bf16[1,1,512,512]{2,3,1,0:T(8,128)(2,1)S(1)} %copy.77) | copy-start | bytes 1572868
  46.3 45.4 %copy-start.43 = (f32[1,512]{1,0:T(1,128)}, f32[1,512]{1,0:T(1,128)S(1)}, u32[]{:S(2)}) copy-start(f32[1,512]{1,0:T(1,128)S(1)} %get-tuple-element.185) | copy-start | bytes 6148
  46.3 45.4 %copy-start.49 = (f32[1,512]{1,0:T(1,128)}, f32[1,512]{1,0:T(1,128)S(1)}, u32[]{:S(2)}) copy-start(f32[1,512]{1,0:T(1,128)S(1)} %get-tuple-element.184) | copy-start | bytes 6148
  46.3 64.1 %copy-start.37 = (f32[1,512]{1,0:T(1,128)}, f32[1,512]{1,0:T(1,128)S(1)}, u32[]{:S(2)}) copy-start(f32[1,512]{1,0:T(1,128)S(1)} %get-tuple-element.182) | copy-start | bytes 6148
  46.3 110.0 %copy-start.46 = (f32[1,1024]{1,0:T(1,128)}, f32[1,1024]{1,0:T(1,128)S(1)}, u32[]{:S(2)}) copy-start(f32[1,1024]{1,0:T(1,128)S(1)} %get-tuple-element.190) | copy-start | bytes 12292
  46.4 62.1 %copy-start.22 = (bf16[512,512]{0,1:T(8,128)(2,1)}, bf16[512,512]{0,1:T(8,128)(2,1)S(1)}, u32[]{:S(2)}) copy-start(bf16[512,512]{0,1:T(8,128)(2,1)S(1)} %collective-permute-done) | copy-start | bytes 1572868
  46.7 45.1 %copy-start.33 = (f32[1024]{0:T(1024)}, f32[1024]{0:T(1024)S(1)}, u32[]{:S(2)}) copy-start(f32[1024]{0:T(1024)S(1)} %broadcast_multiply_fusion.11) | copy-start | bytes 12292
  47.1 44.6 %copy-start.39 = (f32[1024]{0:T(1024)}, f32[1024]{0:T(1024)S(1)}, u32[]{:S(2)}) copy-start(f32[1024]{0:T(1024)S(1)} %add_rsqrt_fusion.3) | copy-start | bytes 12292
  79.2 12.6 %copy-start.6 = (bf16[1024,768]{1,0:T(8,128)(2,1)}, bf16[1024,768]{1,0:T(8,128)(2,1)S(1)}, u32[]{:S(2)}) copy-start(bf16[1024,768]{1,0:T(8,128)(2,1)S(1)} %add_convert_fusion.3.q_ref.k_ref.v_ref) | copy-start | bytes 4718596
  91.7 15.1 %copy-start = (bf16[1024,256]{1,0:T(8,128)(2,1)}, bf16[1024,256]{1,0:T(8,128)(2,1)S(1)}, u32[]{:S(2)}) copy-start(bf16[1024,256]{1,0:T(8,128)(2,1)S(1)} %get-tuple-element.31) | copy-start | bytes 1572868
  94.2 14.2 %copy-start.4 = (bf16[1024,768]{1,0:T(8,128)(2,1)}, bf16[1024,768]{1,0:T(8,128)(2,1)S(1)}, u32[]{:S(2)}) copy-start(bf16[1024,768]{1,0:T(8,128)(2,1)S(1)} %add_convert_fusion.2.q_ref.k_ref.v_ref) | copy-start | bytes 4718596
  110.1 72.5 %copy-start.10 = (f32[1024,512]{0,1:T(8,128)}, f32[1024,512]{0,1:T(8,128)S(1)}, u32[]{:S(2)}) copy-start(f32[1024,512]{0,1:T(8,128)S(1)} %get-tuple-element.220) | copy-start | bytes 6291460
  110.1 59.4 %copy-start.31 = (f32[1024]{0:T(1024)}, f32[1024]{0:T(1024)S(1)}, u32[]{:S(2)}) copy-start(f32[1024]{0:T(1024)S(1)} %broadcast_multiply_fusion.10) | copy-start | bytes 12292
  110.4 59.1 %copy-start.35 = (f32[1024]{0:T(1024)}, f32[1024]{0:T(1024)S(1)}, u32[]{:S(2)}) copy-start(f32[1024]{0:T(1024)S(1)} %add_rsqrt_fusion.2) | copy-start | bytes 12292
  110.8 60.0 %copy-start.28 = (bf16[1024,512]{0,1:T(8,128)(2,1)}, bf16[1024,512]{0,1:T(8,128)(2,1)S(1)}, u32[]{:S(2)}) copy-start(bf16[1024,512]{0,1:T(8,128)(2,1)S(1)} %add_convert_fusion.7) | copy-start | bytes 3145732
  156.3 13.2 %copy-start.59 = (bf16[2048,2048]{1,0:T(8,128)(2,1)S(1)}, bf16[2048,2048]{1,0:T(8,128)(2,1)}, u32[]{:S(2)}) copy-start(bf16[2048,2048]{1,0:T(8,128)(2,1)} %all-gather.7.cloned.1.call-done) | copy-start | bytes 25165828
  183.9 125.5 %copy-start.16 = (bf16[1024,512]{0,1:T(8,128)(2,1)}, bf16[1024,512]{0,1:T(8,128)(2,1)S(1)}, u32[]{:S(2)}) copy-start(bf16[1024,512]{0,1:T(8,128)(2,1)S(1)} %get-tuple-element.224) | copy-start | bytes 3145732
  214.4 58.5 %copy-start.8 = (f32[1024,512]{0,1:T(8,128)}, f32[1024,512]{0,1:T(8,128)S(1)}, u32[]{:S(2)}) copy-start(f32[1024,512]{0,1:T(8,128)S(1)} %get-tuple-element.226) | copy-start | bytes 6291460
  215.0 26.7 %copy-start.27 = (bf16[1,1,512,512]{2,3,1,0:T(8,128)(2,1)S(1)}, bf16[1,1,512,512]{2,3,1,0:T(8,128)(2,1)}, u32[]{:S(2)}) copy-start(bf16[1,1,512,512]{2,3,1,0:T(8,128)(2,1)} %copy.83) | copy-start | bytes 1572868
  347.2 250.0 %reduce-scatter.3.cloned.1.call-start = ((), (), s32[]{:S(2)}) async-start(), calls=%async_computation.4 | async-start | bytes 6488064 | tf_op jit(solution)/shard_map/reduce_scatter | solution.py:792
  371.2 16.8 %copy-start.5 = (bf16[1024,768]{1,0:T(8,128)(2,1)S(1)}, bf16[1024,768]{1,0:T(8,128)(2,1)}, u32[]{:S(2)}) copy-start(bf16[1024,768]{1,0:T(8,128)(2,1)} %copy-done.4) | copy-start | bytes 4718596
  388.0 16.3 %copy-start.29 = (bf16[1024,512]{0,1:T(8,128)(2,1)S(1)}, bf16[1024,512]{0,1:T(8,128)(2,1)}, u32[]{:S(2)}) copy-start(bf16[1024,512]{0,1:T(8,128)(2,1)} %copy-done.28) | copy-start | bytes 3145732
  450.6 10.6 %copy-start.42 = (f32[3072]{0:T(1024)S(1)}, f32[3072]{0:T(1024)}, u32[]{:S(2)}) copy-start(f32[3072]{0:T(1024)} %custom-call.1) | copy-start | bytes 36868
  450.6 10.7 %copy-start.41 = (f32[3072]{0:T(1024)S(1)}, f32[3072]{0:T(1024)}, u32[]{:S(2)}) copy-start(f32[3072]{0:T(1024)} %custom-call) | copy-start | bytes 36868
  450.6 58.4 %copy-start.18 = (bf16[1024,512]{0,1:T(8,128)(2,1)S(1)}, bf16[1024,512]{0,1:T(8,128)(2,1)}, u32[]{:S(2)}) copy-start(bf16[1024,512]{0,1:T(8,128)(2,1)} %copy-done.16) | copy-start | bytes 3145732
  452.0 67.4 %collective-permute-start.5 = (bf16[512,512]{0,1:T(8,128)(2,1)}, bf16[512,512]{0,1:T(8,128)(2,1)}, u32[]{:S(2)}, u32[]{:S(2)}) collective-permute-start(bf16[512,512]{0,1:T(8,128)(2,1)} %get-tuple-element.131), channel_id=1, source_target_pairs={{16,17},{17,16},{18,19},{19,18},{20,21},{21,20},{22,23},{23,22},{2... | collective-permute-start | bytes 1572872 | tf_op jit(solution)/shard_map/ppermute | solution.py:654
  453.4 71.4 %collective-permute-start.6 = (bf16[512,512]{0,1:T(8,128)(2,1)}, bf16[512,512]{0,1:T(8,128)(2,1)}, u32[]{:S(2)}, u32[]{:S(2)}) collective-permute-start(bf16[512,512]{0,1:T(8,128)(2,1)} %get-tuple-element.134), channel_id=1, source_target_pairs={{0,1},{1,0},{2,3},{3,2},{4,5},{5,4},{6,7},{7,6},{8,9},{9,8},{10,11... | collective-permute-start | bytes 1572872 | tf_op jit(solution)/shard_map/ppermute | solution.py:654
  456.8 71.5 %collective-permute-start.7 = (bf16[512,512]{0,1:T(8,128)(2,1)}, bf16[512,512]{0,1:T(8,128)(2,1)}, u32[]{:S(2)}, u32[]{:S(2)}) collective-permute-start(bf16[512,512]{0,1:T(8,128)(2,1)} %get-tuple-element.130), channel_id=1, source_target_pairs={{0,16},{1,17},{2,18},{3,19},{4,20},{5,21},{6,22},{7,23},{8,24},{9,... | collective-permute-start | bytes 1572872 | tf_op jit(solution)/shard_map/ppermute | solution.py:654
  459.9 68.4 %collective-permute-start.8 = (bf16[512,512]{0,1:T(8,128)(2,1)S(1)}, bf16[512,512]{0,1:T(8,128)(2,1)}, u32[]{:S(2)}, u32[]{:S(2)}) collective-permute-start(bf16[512,512]{0,1:T(8,128)(2,1)S(1)} %get-tuple-element.133), channel_id=1, source_target_pairs={{16,0},{17,1},{18,2},{19,3},{20,4},{21,5},{22,6},{23,7},{24,8},{25... | collective-permute-start | bytes 1572872 | tf_op jit(solution)/shard_map/ppermute | solution.py:654
  516.0 26.2 %collective-permute-start.10 = (bf16[512,512]{0,1:T(8,128)(2,1)S(1)}, bf16[512,512]{0,1:T(8,128)(2,1)S(1)}, u32[]{:S(2)}, u32[]{:S(2)}) collective-permute-start(bf16[512,512]{0,1:T(8,128)(2,1)S(1)} %get-tuple-element.132), channel_id=1, source_target_pairs={{16,1},{17,0},{18,3},{19,2},{20,5},{21,4},{22,7},{23,6},{24,9},{25... | collective-permute-start | bytes 1572872 | tf_op jit(solution)/shard_map/ppermute | solution.py:654
  519.3 22.8 %collective-permute-start.9 = (bf16[512,512]{0,1:T(8,128)(2,1)S(1)}, bf16[512,512]{0,1:T(8,128)(2,1)S(1)}, u32[]{:S(2)}, u32[]{:S(2)}) collective-permute-start(bf16[512,512]{0,1:T(8,128)(2,1)S(1)} %get-tuple-element.129), channel_id=1, source_target_pairs={{0,17},{1,16},{2,19},{3,18},{4,21},{5,20},{6,23},{7,22},{8,25},{9,... | collective-permute-start | bytes 1572872 | tf_op jit(solution)/shard_map/ppermute | solution.py:654
  524.8 27.1 %collective-permute-start.1 = (bf16[512,512]{0,1:T(8,128)(2,1)}, bf16[512,512]{0,1:T(8,128)(2,1)}, u32[]{:S(2)}, u32[]{:S(2)}) collective-permute-start(bf16[512,512]{0,1:T(8,128)(2,1)} %get-tuple-element.144), channel_id=1, source_target_pairs={{0,1},{1,0},{16,17},{17,16},{2,3},{3,2},{18,19},{19,18},{4,5},{5,4... | collective-permute-start | bytes 1572872 | tf_op jit(solution)/shard_map/ppermute | solution.py:654
  528.3 24.5 %collective-permute-start.2 = (bf16[512,512]{0,1:T(8,128)(2,1)}, bf16[512,512]{0,1:T(8,128)(2,1)}, u32[]{:S(2)}, u32[]{:S(2)}) collective-permute-start(bf16[512,512]{0,1:T(8,128)(2,1)} %get-tuple-element.143), channel_id=1, source_target_pairs={{0,16},{1,17},{16,0},{17,1},{2,18},{3,19},{18,2},{19,3},{4,20},{5,... | collective-permute-start | bytes 1572872 | tf_op jit(solution)/shard_map/ppermute | solution.py:654
  528.4 35.6 %collective-permute-start.3 = (bf16[512,512]{0,1:T(8,128)(2,1)}, bf16[512,512]{0,1:T(8,128)(2,1)}, u32[]{:S(2)}, u32[]{:S(2)}) collective-permute-start(bf16[512,512]{0,1:T(8,128)(2,1)} %get-tuple-element.142), channel_id=1, source_target_pairs={{0,17},{1,16},{16,1},{17,0},{2,19},{3,18},{18,3},{19,2},{4,21},{5,... | collective-permute-start | bytes 1572872 | tf_op jit(solution)/shard_map/ppermute | solution.py:654
  598.2 5.7 collective-permute-start.11
  (42 other events, 120.7 us)
Sparse Core Ops, SparseCore 0:
  11.6 65.2 all-gather.4
  80.4 75.8 all-gather.6
  347.3 113.1 reduce-scatter.4
  466.9 130.2 reduce-scatter.2
where the time goes:
time: 618 us; the launch traced here: 613 us
  matrix products  145 us (23%)
  waiting for transfers between devices  135 us (22%)
  Pallas kernels  111 us (18%)
  other arithmetic  83.9 us (14%)
  blocking collectives  72.2 us (12%)
  local copies, waits for them, and re-layouts  25.6 us (4%)
  starting transfers between devices  24.6 us (4%)
  between operations  16 us (3%)
    dot_general x48, matrix products, contract(): lax.dot_general(left, right, (((left_dim,), (right_dim,)), ((), ())), pre...  145 us
    all_gather x2, waiting for transfers between devices, gather_blocks(): full = lax.all_gather(block, EVERY, axis=0, tiled=True)  75.3 us
    pallas_call x4, Pallas kernels, attention_backward(): pl.pallas_call(attention_backward_kernel, grid=(pairs,), in_specs=[column...  60.8 us
    concatenate x2, other arithmetic, reduce_grads(): stacked = jnp.concatenate(first_half + second_half, axis=0)  59.3 us
    pallas_call x4, Pallas kernels, attention_forward(): pl.pallas_call(attention_forward_kernel, grid=(pairs,), in_specs=[column(...  50 us
    psum x1, blocking collectives, on_device_clip(): lax.psum((jnp.stack([whole_first, whole_second]), jnp.stack([split_first,...  46.8 us
    ppermute x9, waiting for transfers between devices, trade(): lax.ppermute(sent, GROUP, [(here, here ^ step) for here in range(count) i...  30.1 us
    reduce_scatter x2, waiting for transfers between devices, reduce_grads(): return lax.psum_scatter(stacked, EVERY, scatter_dimension=0, tiled=True)  28.6 us
  transfers between devices with their start and end apart: 16, of which 8 were waited for; matrix products, arithmetic and copies ran while one was open for 27% of the time, Pallas kernels for 13%

commit v1 on v0

--- a/solution.py
+++ b/solution.py
@@ -1,3 +1,4 @@
+import functools
 import math
 
 import jax
@@ -385,277 +386,599 @@
     )
 
 
-QUERY_BLOCK = 256
-
-
-def attention_forward_kernel(q_ref, k_ref, v_ref, context_ref, lse_ref):
-    frames = q_ref.shape[0]
-    score_scale = 1.0 / math.sqrt(HD)
-    for start in range(0, frames, QUERY_BLOCK):
-        rows = slice(start, start + QUERY_BLOCK)
-        parts = []
-        for head in range(2):
-            lanes = slice(head * HD, (head + 1) * HD)
-            scaled = q_ref[rows, lanes] * jnp.asarray(score_scale, jnp.bfloat16)
-            scores = contract(k_ref[:, lanes], scaled, 1, 1)
-            top = jnp.max(scores, axis=0, keepdims=True)
-            weights = jnp.exp(scores - top)
-            total = jnp.sum(weights, axis=0, keepdims=True)
-            mixed = contract(v_ref[:, lanes], weights.astype(jnp.bfloat16), 0, 0)
-            parts.append(mixed / total)
-            lse_ref[0, head : head + 1, rows] = top + jnp.log(total)
-        pair = jnp.concatenate(parts, axis=0)
-        context_ref[rows, :] = pair.T.astype(jnp.bfloat16)
-
-
-def attention_forward(qkv):
-    frames = qkv.shape[0]
-    width = qkv.shape[1] // 3
-    pairs = width // (2 * HD)
-
-    def column(part):
-        return pl.BlockSpec((frames, 2 * HD), lambda pair: (0, pair + part * pairs))
-
-    return pl.pallas_call(
-        attention_forward_kernel,
-        grid=(pairs,),
-        in_specs=[column(0), column(1), column(2)],
-        out_specs=[
-            pl.BlockSpec((frames, 2 * HD), lambda pair: (0, pair)),
-            pl.BlockSpec((1, 8, frames), lambda pair: (pair, 0, 0)),
-        ],
-        out_shape=[
-            jax.ShapeDtypeStruct((frames, width), jnp.bfloat16),
-            jax.ShapeDtypeStruct((pairs, 8, frames), jnp.float32),
-        ],
-        compiler_params=pltpu.CompilerParams(vmem_limit_bytes=40 * 1024 * 1024),
-        cost_estimate=pl.CostEstimate(
-            flops=4 * frames * frames * width,
-            bytes_accessed=8 * frames * width,
-            transcendentals=frames * frames * width // HD,
-        ),
-        name="attention_forward",
-    )(qkv, qkv, qkv)
-
-
-def attention_backward_kernel(q_ref, k_ref, v_ref, grad_ref, lse_ref, out_ref, bias_ref):
-    frames = q_ref.shape[0]
-    width = out_ref.shape[1] // 3
-    pair_index = pl.program_id(0)
-    score_scale = 1.0 / math.sqrt(HD)
-    grad_keys = [None, None]
-    grad_values = [None, None]
-    query_total = jnp.zeros((1, 2 * HD), jnp.float32)
-
-    def columns(part):
-        return pl.ds(pl.multiple_of(part * width + pair_index * (2 * HD), 2 * HD), 2 * HD)
-
-    for start in range(0, frames, QUERY_BLOCK):
-        rows = slice(start, start + QUERY_BLOCK)
-        parts = []
-        for head in range(2):
-            lanes = slice(head * HD, (head + 1) * HD)
-            keys = k_ref[:, lanes]
-            grads = grad_ref[rows, lanes]
-            scaled = q_ref[rows, lanes] * jnp.asarray(score_scale, jnp.bfloat16)
-            scores = contract(keys, scaled, 1, 1)
-            probs = jnp.exp(scores - lse_ref[0, head : head + 1, rows])
-            grad_probs = contract(v_ref[:, lanes], grads, 1, 1)
-            delta = jnp.sum(probs * grad_probs, axis=0, keepdims=True)
-            low_scores = (probs * (grad_probs - delta)).astype(jnp.bfloat16)
-            value_part = contract(probs.astype(jnp.bfloat16), grads, 1, 0)
-            key_part = contract(low_scores, scaled, 1, 0)
-            grad_values[head] = value_part if start == 0 else grad_values[head] + value_part
-            grad_keys[head] = key_part if start == 0 else grad_keys[head] + key_part
-            parts.append(contract(keys, low_scores, 0, 0))
-        pair = jnp.concatenate(parts, axis=0).T * score_scale
-        query_total = query_total + jnp.sum(pair, axis=0, keepdims=True)
-        out_ref[rows, columns(0)] = pair.astype(jnp.bfloat16)
-    key_pair = jnp.concatenate(grad_keys, axis=1)
-    value_pair = jnp.concatenate(grad_values, axis=1)
-    out_ref[:, columns(1)] = key_pair.astype(jnp.bfloat16)
-    out_ref[:, columns(2)] = value_pair.astype(jnp.bfloat16)
-    bias_ref[0:1, columns(0)] = query_total
-    bias_ref[0:1, columns(2)] = jnp.sum(value_pair, axis=0, keepdims=True)
-
-
-def attention_backward(qkv, grad_context, lse):
-    frames = qkv.shape[0]
-    width = qkv.shape[1] // 3
-    pairs = width // (2 * HD)
-
-    def column(part):
-        return pl.BlockSpec((frames, 2 * HD), lambda pair: (0, pair + part * pairs))
-
-    return pl.pallas_call(
-        attention_backward_kernel,
-        grid=(pairs,),
-        in_specs=[
-            column(0),
-            column(1),
-            column(2),
-            column(0),
-            pl.BlockSpec((1, 8, frames), lambda pair: (pair, 0, 0)),
-        ],
-        out_specs=[
-            pl.BlockSpec((frames, 3 * width), lambda pair: (0, 0)),
-            pl.BlockSpec((8, 3 * width), lambda pair: (0, 0)),
-        ],
-        out_shape=[
-            jax.ShapeDtypeStruct((frames, 3 * width), jnp.bfloat16),
-            jax.ShapeDtypeStruct((8, 3 * width), jnp.float32),
-        ],
-        compiler_params=pltpu.CompilerParams(vmem_limit_bytes=40 * 1024 * 1024),
-        cost_estimate=pl.CostEstimate(
-            flops=10 * frames * frames * width,
-            bytes_accessed=14 * frames * width,
-            transcendentals=frames * frames * width // HD,
-        ),
-        name="attention_backward",
-    )(qkv, qkv, qkv, grad_context, lse)
-
-
-def cut_block(block, width, hidden):
-    edge = 4 * width
-    return (
-        block[:, : 3 * width],
-        block[:, 3 * width : edge],
-        block[:, edge : edge + hidden],
-        block[:, edge + hidden :],
-    )
-
-
-def clip_forward(values, blocks, params):
-    (
-        gain_one,
-        shift_one,
-        qkv_bias,
-        proj_bias,
-        gain_two,
-        shift_two,
-        up_bias,
-        down_bias,
-    ) = params
-    centered_one, inv_one, normed_one = norm_forward(values, gain_one, shift_one)
-    qkv_parts, contexts, lses, pre_acts, activated = [], [], [], [], []
-    attended = proj_bias
-    for (qkv_full, proj_turned, up_full, down_turned), bias in zip(blocks, qkv_bias):
-        qkv = (contract(normed_one, qkv_full, 1, 0) + bias).astype(jnp.bfloat16)
-        context, lse = attention_forward(qkv)
-        attended = attended + contract(context, proj_turned, 1, 1)
-        qkv_parts.append(qkv)
-        contexts.append(context)
-        lses.append(lse)
-    hidden = values + attended
-    centered_two, inv_two, normed_two = norm_forward(hidden, gain_two, shift_two)
-    output = hidden + down_bias
-    for (qkv_full, proj_turned, up_full, down_turned), bias in zip(blocks, up_bias):
-        pre_act = contract(normed_two, up_full, 1, 0) + bias
-        active = exact_gelu(pre_act).astype(jnp.bfloat16)
-        output = output + contract(active, down_turned, 1, 1)
-        pre_acts.append(pre_act)
-        activated.append(active)
-    kept = (
-        centered_one,
-        inv_one,
-        normed_one,
-        qkv_parts,
-        contexts,
-        lses,
-        centered_two,
-        inv_two,
-        normed_two,
-        pre_acts,
-        activated,
-    )
-    return (output, kept)
-
-
-def clip_backward(grad_out, kept, blocks, params):
-    gain_one, gain_two = (params[0], params[4])
-    (
-        centered_one,
-        inv_one,
-        normed_one,
-        qkv_parts,
-        contexts,
-        lses,
-        centered_two,
-        inv_two,
-        normed_two,
-        pre_acts,
-        activated,
-    ) = kept
-    grad_down_bias = jnp.sum(grad_out, axis=0)
-    down_grad = grad_out.astype(jnp.bfloat16)
-    grad_normed_two = 0.0
-    up_biases, early, late, query_biases, value_biases = [], [], [], [], []
-    for (qkv_full, proj_turned, up_full, down_turned), pre_act, active in zip(
-        blocks, pre_acts, activated
-    ):
-        grad_down = contract(down_grad, active, 0, 0)
-        grad_act = contract(down_grad, down_turned, 1, 0)
-        grad_pre = jax.vjp(exact_gelu, pre_act)[1](grad_act)[0]
-        up_biases.append(jnp.sum(grad_pre, axis=0))
-        grad_pre_low = grad_pre.astype(jnp.bfloat16)
-        grad_up = contract(normed_two, grad_pre_low, 0, 0)
-        grad_normed_two = grad_normed_two + contract(grad_pre_low, up_full, 1, 1)
-        early.append((grad_up.astype(jnp.bfloat16), grad_down.astype(jnp.bfloat16)))
-    grad_hidden_norm, grad_gain_two, grad_shift_two = norm_backward(
-        grad_normed_two, centered_two, inv_two, gain_two
-    )
-    grad_hidden = grad_out + grad_hidden_norm
-    grad_proj_bias = jnp.sum(grad_hidden, axis=0)
-    proj_grad = grad_hidden.astype(jnp.bfloat16)
-    grad_normed_one = 0.0
-    for (qkv_full, proj_turned, up_full, down_turned), qkv, context, lse in zip(
-        blocks, qkv_parts, contexts, lses
-    ):
-        width = context.shape[1]
-        grad_proj = contract(proj_grad, context, 0, 0)
-        grad_context = contract(proj_grad, proj_turned, 1, 0).astype(jnp.bfloat16)
-        grad_qkv_low, bias_rows = attention_backward(qkv, grad_context, lse)
-        query_biases.append(bias_rows[0, :width])
-        value_biases.append(bias_rows[0, 2 * width :])
-        grad_qkv = contract(normed_one, grad_qkv_low, 0, 0)
-        grad_normed_one = grad_normed_one + contract(grad_qkv_low, qkv_full, 1, 1)
-        late.append((grad_qkv.astype(jnp.bfloat16), grad_proj.astype(jnp.bfloat16)))
-    grad_in_norm, grad_gain_one, grad_shift_one = norm_backward(
-        grad_normed_one, centered_one, inv_one, gain_one
-    )
-    grad_in = grad_hidden + grad_in_norm
-    whole = jnp.concatenate(
-        [
-            grad_gain_one,
-            grad_shift_one,
-            grad_proj_bias,
-            grad_gain_two,
-            grad_shift_two,
-            grad_down_bias,
-        ]
-    )
-    split = jnp.stack(
-        [jnp.concatenate(part) for part in zip(query_biases, value_biases, up_biases)]
-    )
-    return (grad_in, early, late, whole, split)
-
-
+TILE = 256
+LANES = 2 * HD
+VMEM_BYTES = 60 * 1024 * 1024
 GROUP = ("pipe", "col")
 EVERY = ("pipe", "col", "row")
-
-
-def trade(pieces, place, targets):
+ERFC_SCALE = 0.4
+ERFC_TERMS = (
+    0.23192221664065504,
+    0.1618227850291895,
+    0.4682761333792345,
+    -0.37091039694171485,
+    0.7091488547855423,
+    -0.20025962054546065,
+)
+
+
+def gelu_and_slope(values):
+    size = jnp.abs(values) * math.sqrt(0.5)
+    turn = 1.0 / (1.0 + ERFC_SCALE * size)
+    series = ERFC_TERMS[-1]
+    for term in ERFC_TERMS[-2::-1]:
+        series = series * turn + term
+    bell = jnp.exp(-(size * size))
+    tail = 0.5 * (series * turn * bell)
+    below = jnp.where(values >= 0.0, 1.0 - tail, tail)
+    return (values * below, below + values * bell * (1.0 / math.sqrt(2.0 * math.pi)))
+
+
+def norm_rows(values):
+    centered = values - jnp.mean(values, axis=-1, keepdims=True)
+    inv_std = lax.rsqrt(jnp.mean(centered * centered, axis=-1, keepdims=True) + epsilon)
+    return (centered * inv_std, inv_std)
+
+
+def norm_rows_backward(grad, centered, inv_std, gain):
+    scaled = grad * gain
+    first = jnp.mean(scaled, axis=-1, keepdims=True)
+    second = jnp.mean(scaled * centered, axis=-1, keepdims=True)
+    return inv_std * (scaled - first - centered * second)
+
+
+def tile_rows(index):
+    return pl.ds(pl.multiple_of(index * TILE, TILE), TILE)
+
+
+def lane_block(start):
+    return pl.ds(pl.multiple_of(start, LANES), LANES)
+
+
+class Sizes:
+    def __init__(self, frames, features, width, hidden):
+        self.frames = frames
+        self.features = features
+        self.width = width
+        self.hidden = hidden
+        self.tiles = frames // TILE
+        self.pairs = 2 * width // LANES
+        self.tails = 6 * features
+        self.tail = 2 * width + hidden
+        self.vector = self.tails + self.tail
+        self.sums = self.tails + 2 * self.tail
+
+    def pair_base(self, pair):
+        per = self.width // LANES
+        part = pair // per
+        return part * (3 * self.width) + (pair % per) * LANES
+
+
+def attention_forward(sizes, qkv, context, lse):
+    width = sizes.width
+    score_scale = 1.0 / math.sqrt(HD)
+
+    def one_pair(pair, carry):
+        base = sizes.pair_base(pair)
+        for start in range(0, sizes.frames, TILE):
+            rows = slice(start, start + TILE)
+            query_pair = qkv[rows, lane_block(base)]
+            key_pair = qkv[:, lane_block(base + width)]
+            value_pair = qkv[:, lane_block(base + 2 * width)]
+            parts = []
+            for head in range(2):
+                lanes = slice(head * HD, (head + 1) * HD)
+                scaled = query_pair[:, lanes] * jnp.asarray(score_scale, jnp.bfloat16)
+                scores = contract(key_pair[:, lanes], scaled, 1, 1)
+                top = jnp.max(scores, axis=0, keepdims=True)
+                weights = jnp.exp(scores - top)
+                total = jnp.sum(weights, axis=0, keepdims=True)
+                mixed = contract(value_pair[:, lanes], weights.astype(jnp.bfloat16), 0, 0)
+                parts.append(mixed / total)
+                lse[pair, head : head + 1, rows] = top + jnp.log(total)
+            both = jnp.concatenate(parts, axis=0)
+            context[rows, lane_block(pair * LANES)] = both.T.astype(jnp.bfloat16)
+        return carry
+
+    lax.fori_loop(0, sizes.pairs, one_pair, 0)
+
+
+def attention_backward(sizes, qkv, grad_context, lse, add_query_bias, add_value_bias):
+    width = sizes.width
+    score_scale = 1.0 / math.sqrt(HD)
+
+    def one_pair(pair, carry):
+        base = sizes.pair_base(pair)
+        key_pair = qkv[:, lane_block(base + width)]
+        value_pair = qkv[:, lane_block(base + 2 * width)]
+        grad_keys = [None, None]
+        grad_values = [None, None]
+        query_total = jnp.zeros((1, LANES), jnp.float32)
+        for start in range(0, sizes.frames, TILE):
+            rows = slice(start, start + TILE)
+            query_pair = qkv[rows, lane_block(base)]
+            grad_pair = grad_context[rows, lane_block(pair * LANES)]
+            parts = []
+            for head in range(2):
+                lanes = slice(head * HD, (head + 1) * HD)
+                keys = key_pair[:, lanes]
+                grads = grad_pair[:, lanes]
+                scaled = query_pair[:, lanes] * jnp.asarray(score_scale, jnp.bfloat16)
+                scores = contract(keys, scaled, 1, 1)
+                probs = jnp.exp(scores - lse[pair, head : head + 1, rows])
+                grad_probs = contract(value_pair[:, lanes], grads, 1, 1)
+                delta = jnp.sum(probs * grad_probs, axis=0, keepdims=True)
+                low_scores = (probs * (grad_probs - delta)).astype(jnp.bfloat16)
+                value_part = contract(probs.astype(jnp.bfloat16), grads, 1, 0)
+                key_part = contract(low_scores, scaled, 1, 0)
+                grad_values[head] = value_part if start == 0 else grad_values[head] + value_part
+                grad_keys[head] = key_part if start == 0 else grad_keys[head] + key_part
+                parts.append(contract(keys, low_scores, 0, 0))
+            turned = jnp.concatenate(parts, axis=0).T * score_scale
+            query_total = query_total + jnp.sum(turned, axis=0, keepdims=True)
+            qkv[rows, lane_block(base)] = turned.astype(jnp.bfloat16)
+        key_grad = jnp.concatenate(grad_keys, axis=1)
+        value_grad = jnp.concatenate(grad_values, axis=1)
+        qkv[:, lane_block(base + width)] = key_grad.astype(jnp.bfloat16)
+        qkv[:, lane_block(base + 2 * width)] = value_grad.astype(jnp.bfloat16)
+        add_query_bias(pair, query_total)
+        add_value_bias(pair, jnp.sum(value_grad, axis=0, keepdims=True))
+        return carry
+
+    lax.fori_loop(0, sizes.pairs, one_pair, 0)
+
+
+def vector_reader(sizes, vectors, layer):
+    features, width = (sizes.features, sizes.width)
+
+    def whole(index):
+        return vectors[2 * layer : 2 * layer + 1, index * features : (index + 1) * features]
+
+    def split(part, start, size):
+        row = 2 * layer + part
+        first = sizes.tails + start
+        return vectors[row : row + 1, first : first + size]
+
+    return (whole, split)
+
+
+def forward_qkv(sizes, layer, values, early, vectors, qkv):
+    features, width = (sizes.features, sizes.width)
+    whole, split = vector_reader(sizes, vectors, layer)
+
+    def one_tile(index, carry):
+        rows = tile_rows(index)
+        centered, unused = norm_rows(values[rows, :].astype(jnp.float32))
+        normed = (centered * whole(0) + whole(1)).astype(jnp.bfloat16)
+        for part in range(2):
+            weights = early.at[2 * layer + part]
+            for kind in range(3):
+                result = contract(normed, weights[:, kind * width : (kind + 1) * width], 1, 0)
+                if kind == 0:
+                    result = result + split(part, 0, width)
+                if kind == 2:
+                    result = result + split(part, width, width)
+                first = (3 * part + kind) * width
+                qkv[rows, first : first + width] = result.astype(jnp.bfloat16)
+        return carry
+
+    lax.fori_loop(0, sizes.tiles, one_tile, 0)
+
+
+def forward_rest(sizes, layer, values, early, late, vectors, context, hidden, active, slope, output):
+    features, width, size = (sizes.features, sizes.width, sizes.hidden)
+    whole, split = vector_reader(sizes, vectors, layer)
+
+    def one_tile(index, carry):
+        rows = tile_rows(index)
+        total = values[rows, :].astype(jnp.float32) + whole(2)
+        for part in range(2):
+            total = total + contract(
+                context[rows, part * width : (part + 1) * width],
+                early[2 * layer + part, :, 3 * width : 4 * width],
+                1,
+                1,
+            )
+        hidden[rows, :] = total
+        centered, unused = norm_rows(total)
+        normed = (centered * whole(3) + whole(4)).astype(jnp.bfloat16)
+        total = total + whole(5)
+        for part in range(2):
+            for start in range(0, size, 512):
+                pre_act = contract(
+                    normed, late[2 * layer + part, :, start : start + 512], 1, 0
+                ) + split(part, 2 * width + start, 512)
+                act, act_slope = gelu_and_slope(pre_act)
+                act = act.astype(jnp.bfloat16)
+                first = part * size + start
+                active[rows, first : first + 512] = act
+                slope[rows, first : first + 512] = act_slope.astype(jnp.bfloat16)
+                total = total + contract(
+                    act, late[2 * layer + part, :, size + start : size + start + 512], 1, 1
+                )
+        output[rows, :] = total.astype(jnp.bfloat16)
+        return carry
+
+    lax.fori_loop(0, sizes.tiles, one_tile, 0)
+
+
+def forward_kernel(
+    sizes,
+    x_ref,
+    early_ref,
+    late_ref,
+    vector_ref,
+    sent_ref,
+    final_ref,
+    lse_ref,
+    qkv_out,
+    context_out,
+    hidden_out,
+    active_out,
+    slope_out,
+    qkv,
+    context,
+    hidden,
+    active,
+    slope,
+    sems,
+):
+    copies = []
+
+    def save(source, target, layer, number):
+        copy = pltpu.make_async_copy(source.at[layer], target.at[layer], sems.at[layer, number])
+        copy.start()
+        copies.append(copy)
+
+    for layer in range(2):
+        values = (x_ref, sent_ref)[layer]
+        output = (sent_ref, final_ref)[layer]
+        forward_qkv(sizes, layer, values, early_ref, vector_ref, qkv.at[layer])
+        save(qkv, qkv_out, layer, 0)
+        attention_forward(sizes, qkv.at[layer], context.at[layer], lse_ref.at[layer])
+        save(context, context_out, layer, 1)
+        forward_rest(
+            sizes,
+            layer,
+            values,
+            early_ref,
+            late_ref,
+            vector_ref,
+            context.at[layer],
+            hidden.at[layer],
+            active.at[layer],
+            slope.at[layer],
+            output,
+        )
+        save(hidden, hidden_out, layer, 2)
+        save(active, active_out, layer, 3)
+        save(slope, slope_out, layer, 4)
+    for copy in copies:
+        copy.wait()
+
+
+def saved_shapes(sizes):
+    frames, features = (sizes.frames, sizes.features)
+    return [
+        ((2, frames, 6 * sizes.width), jnp.bfloat16),
+        ((2, frames, 2 * sizes.width), jnp.bfloat16),
+        ((2, frames, features), jnp.float32),
+        ((2, frames, 2 * sizes.hidden), jnp.bfloat16),
+        ((2, frames, 2 * sizes.hidden), jnp.bfloat16),
+    ]
+
+
+def run_forward(sizes, values, early, late, vectors):
+    frames, features = (sizes.frames, sizes.features)
+    vmem = pl.BlockSpec(memory_space=pltpu.VMEM)
+    hbm = pl.BlockSpec(memory_space=pl.ANY)
+    saved = saved_shapes(sizes)
+    return pl.pallas_call(
+        functools.partial(forward_kernel, sizes),
+        in_specs=[vmem] * 4,
+        out_specs=[vmem] * 3 + [hbm] * 5,
+        out_shape=[
+            jax.ShapeDtypeStruct((frames, features), jnp.bfloat16),
+            jax.ShapeDtypeStruct((frames, features), jnp.bfloat16),
+            jax.ShapeDtypeStruct((2, sizes.pairs, 2, frames), jnp.float32),
+        ]
+        + [jax.ShapeDtypeStruct(shape, dtype) for shape, dtype in saved],
+        scratch_shapes=[pltpu.VMEM(shape, dtype) for shape, dtype in saved]
+        + [pltpu.SemaphoreType.DMA((2, 5))],
+        compiler_params=pltpu.CompilerParams(vmem_limit_bytes=VMEM_BYTES),
+        name="layers_forward",
+    )(values, early, late, vectors)
+
+
+def add_row(sums, layer, start, value):
+    where = (slice(layer, layer + 1), slice(start, start + value.shape[1]))
+    sums[where] = sums[where] + value
+
+
+def column_sum(values):
+    return jnp.sum(values, axis=0, keepdims=True)
+
+
+def backward_mlp(
+    sizes, layer, hidden, active, slope, early, late, vectors, grad, sums, normed_t, grad_t, grad_late
+):
+    features, width, size = (sizes.features, sizes.width, sizes.hidden)
+    whole, split = vector_reader(sizes, vectors, layer)
+
+    def one_tile(index, carry):
+        rows = tile_rows(index)
+        grad_out = grad[rows, :]
+        add_row(sums, layer, 5 * features, column_sum(grad_out))
+        grad_low = grad_out.astype(jnp.bfloat16)
+        grad_t[:, rows] = grad_low.T
+        centered, inv_std = norm_rows(hidden[rows, :])
+        normed_t[:, rows] = (centered * whole(3) + whole(4)).astype(jnp.bfloat16).T
+        grad_normed = jnp.zeros((TILE, features), jnp.float32)
+        for part in range(2):
+            for start in range(0, size, 512):
+                first = part * size + start
+                grad_act = contract(
+                    grad_low, late[2 * layer + part, :, size + start : size + start + 512], 1, 0
+                )
+                grad_pre = grad_act * slope[rows, first : first + 512].astype(jnp.float32)
+                add_row(
+                    sums,
+                    layer,
+                    sizes.tails + part * sizes.tail + 2 * width + start,
+                    column_sum(grad_pre),
+                )
+                low = grad_pre.astype(jnp.bfloat16)
+                slope[rows, first : first + 512] = low
+                grad_normed = grad_normed + contract(
+                    low, late[2 * layer + part, :, start : start + 512], 1, 1
+                )
+        add_row(sums, layer, 3 * features, column_sum(grad_normed * centered))
+        add_row(sums, layer, 4 * features, column_sum(grad_normed))
+        grad_hidden = grad_out + norm_rows_backward(grad_normed, centered, inv_std, whole(3))
+        add_row(sums, layer, 2 * features, column_sum(grad_hidden))
+        grad[rows, :] = grad_hidden
+        return carry
+
+    lax.fori_loop(0, sizes.tiles, one_tile, 0)
+    for part in range(2):
+        for start in range(0, size, 256):
+            first = part * size + start
+            up = contract(normed_t[...], slope[:, first : first + 256], 1, 0)
+            grad_late[part, :, start : start + 256] = up.astype(jnp.bfloat16)
+            down = contract(grad_t[...], active[:, first : first + 256], 1, 0)
+            grad_late[part, :, size + start : size + start + 256] = down.astype(jnp.bfloat16)
+
+
+def backward_attention(
+    sizes,
+    layer,
+    values,
+    qkv,
+    context,
+    lse,
+    early,
+    vectors,
+    grad,
+    sums,
+    normed_t,
+    grad_t,
+    grad_context,
+    grad_early,
+    grad_in,
+):
+    features, width = (sizes.features, sizes.width)
+    whole, split = vector_reader(sizes, vectors, layer)
+
+    def to_context(index, carry):
+        rows = tile_rows(index)
+        low = grad[rows, :].astype(jnp.bfloat16)
+        grad_t[:, rows] = low.T
+        for part in range(2):
+            grad_context[rows, part * width : (part + 1) * width] = contract(
+                low, early[2 * layer + part, :, 3 * width : 4 * width], 1, 0
+            ).astype(jnp.bfloat16)
+        return carry
+
+    lax.fori_loop(0, sizes.tiles, to_context, 0)
+    per = width // LANES
+
+    def add_bias(offset):
+        def add(pair, value):
+            start = sizes.tails + (pair // per) * sizes.tail + offset + (pair % per) * LANES
+            where = (slice(layer, layer + 1), lane_block(start))
+            sums[where] = sums[where] + value
+
+        return add
+
+    attention_backward(sizes, qkv, grad_context, lse, add_bias(0), add_bias(width))
+
+    def to_input(index, carry):
+        rows = tile_rows(index)
+        grad_normed = jnp.zeros((TILE, features), jnp.float32)
+        for part in range(2):
+            grad_normed = grad_normed + contract(
+                qkv[rows, part * 3 * width : (part + 1) * 3 * width],
+                early[2 * layer + part, :, : 3 * width],
+                1,
+                1,
+            )
+        centered, inv_std = norm_rows(values[rows, :].astype(jnp.float32))
+        normed_t[:, rows] = (centered * whole(0) + whole(1)).astype(jnp.bfloat16).T
+        add_row(sums, layer, 0, column_sum(grad_normed * centered))
+        add_row(sums, layer, features, column_sum(grad_normed))
+        low = (
+            grad[rows, :] + norm_rows_backward(grad_normed, centered, inv_std, whole(0))
+        ).astype(jnp.bfloat16)
+        grad_in[rows, :] = low
+        grad[rows, :] = low.astype(jnp.float32)
+        return carry
+
+    lax.fori_loop(0, sizes.tiles, to_input, 0)
+    for part in range(2):
+        for kind in range(3):
+            first = (3 * part + kind) * width
+            result = contract(normed_t[...], qkv[:, first : first + width], 1, 0)
+            grad_early[part, :, kind * width : (kind + 1) * width] = result.astype(jnp.bfloat16)
+        result = contract(grad_t[...], context[:, part * width : (part + 1) * width], 1, 0)
+        grad_early[part, :, 3 * width :] = result.astype(jnp.bfloat16)
+
+
+def backward_kernel(
+    sizes,
+    live_ref,
+    cot_ref,
+    x_ref,
+    sent_ref,
+    early_ref,
+    late_ref,
+    vector_ref,
+    lse_ref,
+    qkv_in,
+    context_in,
+    hidden_in,
+    active_in,
+    slope_in,
+    mid_ref,
+    start_ref,
+    sums,
+    grad_early_out,
+    grad_late_out,
+    qkv,
+    context,
+    hidden,
+    active,
+    slope,
+    early,
+    late,
+    grad,
+    normed_t,
+    grad_t,
+    grad_context,
+    grad_early,
+    grad_late,
+    sems,
+):
+    def load(source, target, layer, number):
+        copy = pltpu.make_async_copy(source.at[layer], target, sems.at[layer, number])
+        copy.start()
+        return copy
+
+    def store(source, target, layer, number):
+        copy = pltpu.make_async_copy(
+            source, target.at[pl.ds(2 * layer, 2)], sems.at[layer, number]
+        )
+        copy.start()
+        return copy
+
+    def load_pair(source, target, layer, number):
+        copy = pltpu.make_async_copy(
+            source.at[pl.ds(2 * layer, 2)], target.at[pl.ds(2 * layer, 2)], sems.at[layer, number]
+        )
+        copy.start()
+        return copy
+
+    sums[...] = jnp.zeros_like(sums)
+    late_copies = [load_pair(late_ref, late, layer, 5) for layer in (1, 0)]
+    early_copies = [load_pair(early_ref, early, layer, 6) for layer in (1, 0)]
+    grad[...] = cot_ref[...].astype(jnp.float32) * live_ref[0, 0]
+    stores = []
+    for step, layer in enumerate((1, 0)):
+        mlp = [
+            load(hidden_in, hidden, layer, 0),
+            load(slope_in, slope, layer, 1),
+            load(active_in, active, layer, 2),
+        ]
+        attention = [load(qkv_in, qkv, layer, 3), load(context_in, context, layer, 4)]
+        late_copies[step].wait()
+        for copy in mlp:
+            copy.wait()
+        backward_mlp(
+            sizes,
+            layer,
+            hidden,
+            active,
+            slope,
+            early,
+            late,
+            vector_ref,
+            grad,
+            sums,
+            normed_t,
+            grad_t,
+            grad_late.at[pl.ds(2 * layer, 2)],
+        )
+        stores.append(
+            store(grad_late.at[pl.ds(2 * layer, 2)], grad_late_out, layer, 7)
+        )
+        early_copies[step].wait()
+        for copy in attention:
+            copy.wait()
+        backward_attention(
+            sizes,
+            layer,
+            (x_ref, sent_ref)[layer],
+            qkv,
+            context,
+            lse_ref.at[layer],
+            early,
+            vector_ref,
+            grad,
+            sums,
+            normed_t,
+            grad_t,
+            grad_context,
+            grad_early.at[pl.ds(2 * layer, 2)],
+            (start_ref, mid_ref)[layer],
+        )
+        stores.append(
+            store(grad_early.at[pl.ds(2 * layer, 2)], grad_early_out, layer, 8)
+        )
+    for copy in stores:
+        copy.wait()
+
+
+def run_backward(sizes, live, cot, values, sent, early, late, vectors, lse, saved):
+    frames, features = (sizes.frames, sizes.features)
+    vmem = pl.BlockSpec(memory_space=pltpu.VMEM)
+    hbm = pl.BlockSpec(memory_space=pl.ANY)
+    smem = pl.BlockSpec(memory_space=pltpu.SMEM)
+    low = jnp.bfloat16
+    return pl.pallas_call(
+        functools.partial(backward_kernel, sizes),
+        in_specs=[smem, vmem, vmem, vmem, hbm, hbm, vmem, vmem] + [hbm] * 5,
+        out_specs=[vmem, vmem, vmem, hbm, hbm],
+        out_shape=[
+            jax.ShapeDtypeStruct((frames, features), low),
+            jax.ShapeDtypeStruct((frames, features), low),
+            jax.ShapeDtypeStruct((2, sizes.sums), jnp.float32),
+            jax.ShapeDtypeStruct(early.shape, low),
+            jax.ShapeDtypeStruct(late.shape, low),
+        ],
+        scratch_shapes=[pltpu.VMEM(shape[1:], dtype) for shape, dtype in saved_shapes(sizes)]
+        + [
+            pltpu.VMEM(early.shape, low),
+            pltpu.VMEM(late.shape, low),
+            pltpu.VMEM((frames, features), jnp.float32),
+            pltpu.VMEM((features, frames), low),
+            pltpu.VMEM((features, frames), low),
+            pltpu.VMEM((frames, 2 * sizes.width), low),
+            pltpu.VMEM(early.shape, low),
+            pltpu.VMEM(late.shape, low),
+            pltpu.SemaphoreType.DMA((2, 9)),
+        ],
+        compiler_params=pltpu.CompilerParams(vmem_limit_bytes=VMEM_BYTES),
+        name="layers_backward",
+    )(live, cot, values, sent, early, late, vectors, lse, *saved)
+
+
+def trade(pieces, place):
     count = len(pieces)
     stacked = jnp.stack(pieces)
     taken = [lax.dynamic_index_in_dim(stacked, place, 0, keepdims=False)]
     for step in range(1, count):
         sent = lax.dynamic_index_in_dim(stacked, place ^ step, 0, keepdims=False)
         taken.append(
-            lax.ppermute(
-                sent,
-                GROUP,
-                [(here, here ^ step) for here in range(count) if here ^ step in targets],
-            )
+            lax.ppermute(sent, GROUP, [(here, here ^ step) for here in range(count)])
         )
     return taken
 
@@ -672,9 +995,7 @@
 
 def swap_columns(own, other, col):
     got = lax.ppermute(other, "col", [(0, 1), (1, 0)])
-    return jnp.where(
-        col == 0, jnp.concatenate([own, got]), jnp.concatenate([got, own])
-    )
+    return jnp.where(col == 0, jnp.concatenate([own, got]), jnp.concatenate([got, own]))
 
 
 def gather_blocks(block):
@@ -705,12 +1026,13 @@
     width, hidden_width = (qkv_weight.shape[3], up_weight.shape[2])
     features = inputs.shape[3]
     half = inputs.shape[2]
+    sizes = Sizes(2 * half, features, width, hidden_width)
     early_block = jnp.concatenate(
         [qkv_weight[0, 0], qkv_weight[0, 1], qkv_weight[0, 2], proj_weight[0].T], axis=1
     )
     late_block = jnp.concatenate([up_weight[0], down_weight[0].T], axis=1)
-    early_full = gather_blocks(early_block)
-    late_full = gather_blocks(late_block)
+    early = gather_blocks(early_block)
+    late = gather_blocks(late_block)
     vectors = lax.all_gather(
         jnp.concatenate(
             [
@@ -729,116 +1051,51 @@
         axis=0,
         tiled=False,
     )
-    blocks, params = ([], [])
-    for layer in range(2):
-        blocks.append(
-            [
-                (
-                    early_full[2 * layer + part][:, : 3 * width],
-                    early_full[2 * layer + part][:, 3 * width :],
-                    late_full[2 * layer + part][:, :hidden_width],
-                    late_full[2 * layer + part][:, hidden_width:],
-                )
-                for part in range(2)
-            ]
-        )
-        rows = vectors[2 * layer]
-        whole = [rows[index * features : (index + 1) * features] for index in range(6)]
-        tails = [vectors[2 * layer + part][6 * features :] for part in range(2)]
-        params.append(
-            (
-                whole[0],
-                whole[1],
-                [
-                    jnp.concatenate(
-                        [tail[:width], jnp.zeros((width,), jnp.float32), tail[width : 2 * width]]
-                    )
-                    for tail in tails
-                ],
-                whole[2],
-                whole[3],
-                whole[4],
-                [tail[2 * width :] for tail in tails],
-                whole[5],
-            )
-        )
 
     def own_clip(rows):
         own = lax.dynamic_index_in_dim(rows[:, 0], place, 0, keepdims=False)
         other = lax.dynamic_index_in_dim(rows[:, 0], place ^ 1, 0, keepdims=False)
         return swap_columns(own, other, col)
 
-    values = own_clip(inputs).astype(jnp.float32)
-    live_flag = lax.dynamic_index_in_dim(live_clips[:, 0], place, 0, keepdims=False)
-    grad_final = own_clip(cotangent).astype(jnp.float32) * live_flag.astype(jnp.float32)
-    first, kept_first = clip_forward(values, blocks[0], params[0])
-    sent = first.astype(jnp.bfloat16)
-    second, kept_second = clip_forward(sent.astype(jnp.float32), blocks[1], params[1])
-    final = second.astype(jnp.bfloat16)
+    values = own_clip(inputs)
+    cot = own_clip(cotangent)
+    live = lax.dynamic_slice(live_clips, (place, 0), (1, 1)).astype(jnp.float32)
+    sent, final, lse, *saved = run_forward(sizes, values, early, late, vectors)
+    mid, start, sums, grad_early, grad_late = run_backward(
+        sizes, live, cot, values, sent, early, late, vectors, lse, saved
+    )
+    own_early, own_late = [
+        lax.psum_scatter(
+            grads.reshape(-1, grads.shape[2]), EVERY, scatter_dimension=0, tiled=True
+        ).astype(jnp.float32)
+        for grads in (grad_early, grad_late)
+    ]
     states = in_order(
-        trade([sent[:half], sent[half:], final[:half], final[half:]], place, (0, 1, 2, 3)), place
-    )
-
-    def reduce_grads(early, late):
-        quarter = hidden_width // 2
-        first_half = [
-            jnp.concatenate([part[0], part[1], up_part[0][:, :quarter]], axis=1)
-            for part, up_part in zip(late, early)
-        ]
-        second_half = [
-            jnp.concatenate([up_part[0][:, quarter:], up_part[1]], axis=1) for up_part in early
-        ]
-        stacked = jnp.concatenate(first_half + second_half, axis=0)
-        return lax.psum_scatter(stacked, EVERY, scatter_dimension=0, tiled=True)
-
-    grad_mid, early, late, whole_second, split_second = clip_backward(
-        grad_final, kept_second, blocks[1], params[1]
-    )
-    mid_low = grad_mid.astype(jnp.bfloat16)
-    own_second = reduce_grads(early, late)
-    mid_taken = trade([mid_low[:half], mid_low[half:]] * 2, place, (2, 3))
-    grad_start, early, late, whole_first, split_first = clip_backward(
-        mid_low.astype(jnp.float32), kept_first, blocks[0], params[0]
-    )
-    own_first = reduce_grads(early, late)
-    start_low = grad_start.astype(jnp.bfloat16)
-    start_taken = trade([start_low[:half], start_low[half:]] * 2, place, (0, 1))
+        trade([sent[:half], sent[half:], final[:half], final[half:]], place), place
+    )
     grads_in = in_order(
-        [jnp.where(section == 1, mid, start) for mid, start in zip(mid_taken, start_taken)], place
+        trade([start[:half], start[half:], mid[:half], mid[half:]], place), place
     ).astype(jnp.float32)
-    kept_half = jnp.where(section == 0, own_first, own_second)
-    moved = lax.ppermute(
-        jnp.where(section == 0, own_second, own_first), "pipe", [(0, 1), (1, 0)]
-    )
-    packed = jnp.where(
-        section == 0,
-        jnp.concatenate([kept_half, moved], axis=1),
-        jnp.concatenate([moved, kept_half], axis=1),
-    ).astype(jnp.float32)
-    grad_qkv, grad_proj, grad_up, grad_down = cut_block(packed, width, hidden_width)
-    whole_all, split_all = lax.psum(
-        (jnp.stack([whole_first, whole_second]), jnp.stack([split_first, split_second])), EVERY
-    )
-    whole_out = lax.dynamic_index_in_dim(whole_all, section, 0, keepdims=False).reshape(
-        6, 1, features
-    )
-    split_out = lax.dynamic_index_in_dim(split_all, section, 0, keepdims=False)
-    split_out = lax.dynamic_index_in_dim(split_out, col, 0, keepdims=False)
+    sums_all = lax.dynamic_slice(lax.psum(sums, EVERY), (section, 0), (1, sizes.sums))
+    split_out = lax.dynamic_slice(
+        sums_all, (0, sizes.tails + col * sizes.tail), (1, sizes.tail)
+    )
+    whole_out = [sums_all[:, index * features : (index + 1) * features] for index in range(6)]
     return (
         states[None, :, None],
         grads_in[None, :, None],
         whole_out[0],
         whole_out[1],
-        jnp.stack([grad_qkv[:, part * width : (part + 1) * width] for part in range(3)])[None],
-        split_out[None, :width],
-        split_out[None, width : 2 * width],
-        grad_proj.T[None],
+        jnp.stack([own_early[:, part * width : (part + 1) * width] for part in range(3)])[None],
+        split_out[:, :width],
+        split_out[:, width : 2 * width],
+        own_early[:, 3 * width :].T[None],
         whole_out[2],
         whole_out[3],
         whole_out[4],
-        grad_up[None],
-        split_out[None, 2 * width :],
-        grad_down.T[None],
+        own_late[:, :hidden_width][None],
+        split_out[:, 2 * width :],
+        own_late[:, hidden_width:].T[None],
         whole_out[5],
     )
 

time: 618 us -> 674 us (1.091)
  waiting for transfers between devices: 135 us -> 307 us
  matrix products: 145 us -> 0 us
  Pallas kernels: 111 us -> 208 us
  other arithmetic: 83.9 us -> 15.8 us
  blocking collectives: 72.2 us -> 97.5 us
  local copies, waits for them, and re-layouts: 25.6 us -> 10.9 us
  starting transfers between devices: 24.6 us -> 11.6 us
    reduce_scatter x2, waiting for transfers between devices: 28.6 us -> 187 us  [on_device_clip(): lax.psum_scatter(grads.reshape(-1, grads.shape[2]), EVERY, scatter_dimens...]
    dot_general x48 -> x0, matrix products: 145 us -> none  [contract(): lax.dot_general(left, right, (((left_dim,), (right_dim,)), ((), ())), pre...]
    pallas_call x8 -> x2, Pallas kernels: 111 us -> 208 us  [the longest x1 114 us: run_backward(): pl.pallas_call(functools.partial(backward_kernel, sizes), in_specs=[smem,...]
    concatenate x7 -> x0, other arithmetic: 59.3 us -> none  [the longest x2 59.3 us: reduce_grads(): stacked = jnp.concatenate(first_half + second_half, axis=0)]
    all_gather x2, waiting for transfers between devices: 75.3 us -> 107 us  [gather_blocks(): full = lax.all_gather(block, EVERY, axis=0, tiled=True)]
    psum x1, blocking collectives: 46.8 us -> 70.1 us  [on_device_clip(): lax.psum(sums, EVERY)]
    ppermute x10 -> x6, waiting for transfers between devices: 30.7 us -> 11.3 us  [trade(): lax.ppermute(sent, GROUP, [(here, here ^ step) for here in range(count)])]
    ppermute x10 -> x6, starting transfers between devices: 21.4 us -> 8 us  [trade(): lax.ppermute(sent, GROUP, [(here, here ^ step) for here in range(count)])]
  transfers between devices with their start and end apart: 16 -> 12, of which waited for: 8 -> 5; matrix products, arithmetic and copies ran while one was open for 27% -> 3% of each run, Pallas kernels for 13% -> 0%
where the time goes in v1:
time: 674 us; the launch traced here: 666 us
  waiting for transfers between devices  307 us (46%)
  Pallas kernels  208 us (31%)
  blocking collectives  97.5 us (14%)
  other arithmetic  15.8 us (2%)
  between operations  15.4 us (2%)
  starting transfers between devices  11.6 us (2%)
  local copies, waits for them, and re-layouts  10.9 us (2%)
    reduce_scatter x2, waiting for transfers between devices, on_device_clip(): lax.psum_scatter(grads.reshape(-1, grads.shape[2]), EVERY, scatter_dimens...  187 us
    pallas_call x1, Pallas kernels, run_backward(): pl.pallas_call(functools.partial(backward_kernel, sizes), in_specs=[smem,...  114 us
    all_gather x2, waiting for transfers between devices, gather_blocks(): full = lax.all_gather(block, EVERY, axis=0, tiled=True)  107 us
    pallas_call x1, Pallas kernels, run_forward(): pl.pallas_call(functools.partial(forward_kernel, sizes), in_specs=[vmem]...  94.3 us
    psum x1, blocking collectives, on_device_clip(): lax.psum(sums, EVERY)  70.1 us
    all_gather x1, blocking collectives, on_device_clip(): lax.all_gather(jnp.concatenate([first_gain[0], first_shift[0], proj_bias[...  27.5 us
  transfers between devices with their start and end apart: 12, of which 5 were waited for; matrix products, arithmetic and copies ran while one was open for 3% of the time, Pallas kernels for 0%

profile of v1, /device:TPU:0, one launch (start us, length us, event | category | flops | bytes accessed | tf_op | source)
XLA Modules:
  0.0 666.1 jit_solution(8700082950585946306)
XLA Ops:
  7.2 0.8 slice_bitcast_fusion.16
  8.0 1.4 pad_maximum_fusion.5
  9.5 1.7 pad_maximum_fusion.4
  11.4 1.4 dynamic-slice_bitcast_fusion.13
  12.8 3.0 collective-permute-start
  16.0 0.4 collective-permute-start.4
  16.5 27.5 %all-gather.1 = f32[4,1,4608]{2,1,0:T(1,128)S(1)} all-gather(f32[1,1,4608]{2,1,0:T(1,128)S(1)} %reshape.110), channel_id=2, replica_groups=mesh['pipe'=2,'row'=8,'col'=2] {'pipe','col'}, dimensions={0}, use_global_device_ids=true | all-gather | bytes 92160 | tf_op jit(solution)/shard_map/all_gather | solution.py:1036
  44.0 0.7 copy.38
  44.7 0.6 constant_dynamic-slice_fusion.2
  45.9 1.4 maximum_select_fusion.x_ref
  47.4 1.4 maximum_select_fusion.1.cot_ref
  48.8 27.9 %all-gather.5.cloned.1.call-done = bf16[2048,1024]{1,0:T(8,128)(2,1)} async-done(((bf16[64,1024]{1,0:T(8,128)(2,1)}), bf16[2048,1024]{1,0:T(8,128)(2,1)}) %all-gather.5.cloned.1.call-update) | async-done | bytes 4194320 | tf_op jit(solution)/shard_map/all_gather | solution.py:1002
  76.7 79.4 %all-gather.7.cloned.1.call-done = bf16[2048,2048]{1,0:T(8,128)(2,1)} async-done(((bf16[64,2048]{1,0:T(8,128)(2,1)}), bf16[2048,2048]{1,0:T(8,128)(2,1)}) %all-gather.7.cloned.1.call-update) | async-done | bytes 8388624 | tf_op jit(solution)/shard_map/all_gather | solution.py:1002
  156.2 94.3 %layers_forward.1 = (bf16[1024,512]{1,0:T(8,128)(2,1)}, bf16[1024,512]{1,0:T(8,128)(2,1)}, f32[2,4,2,1024]{3,2,1,0:T(2,128)}, bf16[2,1024,1536]{2,1,0:T(8,128)(2...) custom-call(bf16[1024,512]{1,0:T(8,128)(2,1)} %maximum_select_fusion, ...), custom_call_target="tpu_custom_call" | custom-call | tf_op jit(solution)/shard_map/layers_forward/pallas_call | solution.py:676
  250.5 114.0 %layers_backward.1 = (bf16[1024,512]{1,0:T(8,128)(2,1)}, bf16[1024,512]{1,0:T(8,128)(2,1)}, f32[2,6144]{1,0:T(2,128)}, bf16[4,512,1024]{2,1,0:T(8,128)(2,1)}, bf16[4,512,2048]{2,1,0:T(8,128)(2,1)}) custom-call(f32[1,1]{1,0:T(1,128)S(6)} %convert_element_type.19.live_ref, bf16[1024,512]{1,0:T(8,128)(2,1)} %maximum_select_fusion.1.cot_ref, ...), custom_call_target="tpu_custom_call" | custom-call | tf_op jit(solution)/shard_map/layers_backward/pallas_call | solution.py:946
  364.5 0.5 reduce-scatter.5.cloned.1.call-update
  365.1 0.7 copy-done.4
  365.7 0.3 copy-done.5
  366.1 0.1 slice_bitcast_fusion.1
  366.2 0.3 pad_maximum_fusion.2
  366.5 1.0 constant_dynamic-slice_fusion.1
  367.5 1.5 collective-permute-start.5
  368.9 0.6 collective-permute-start.6
  369.5 1.4 collective-permute-start.7
  371.0 0.1 slice_bitcast_fusion.5
  371.1 0.3 pad_maximum_fusion
  371.4 1.2 constant_dynamic-slice_fusion.7
  372.6 1.5 collective-permute-start.1
  374.1 0.6 collective-permute-start.2
  374.7 70.1 %psum.7 = f32[2,6144]{1,0:T(2,128)S(1)} all-reduce(f32[2,6144]{1,0:T(2,128)S(1)} %copy-done.7), channel_id=1, replica_groups=mesh['pipe'=2,'row'=8,'col'=2] {'pipe','col','row'}, use_global_device_ids=true, to_apply=%region_0.1 | all-reduce | flops 12288 | bytes 98304 | tf_op jit(solution)/shard_map/psum | solution.py:1079
  444.7 0.7 dynamic-slice.11
  445.4 2.5 collective-permute-start.3
  447.9 0.6 fusion.1
  448.5 0.7 fusion
  449.2 1.3 pad_maximum_fusion.3
  450.5 0.1 dynamic-slice_bitcast_fusion.3
  450.7 11.2 %collective-permute-done.3 = bf16[512,512]{1,0:T(8,128)(2,1)S(1)} collective-permute-done((bf16[512,512]{1,0:T(8,128)(2,1)}, bf16[512,512]{1,0:T(8,128)(2,1)S(1)}, u32[]{:S(2)}, u32[]{:S(2)}) %collective-permute-start.3) | collective-permute-done | bytes 524320 | tf_op jit(solution)/shard_map/ppermute | solution.py:981
  461.9 1.5 pad_maximum_fusion.1
  463.4 0.1 constant_dynamic-slice_fusion.6
  463.6 1.6 maximum_bitcast_fusion
  465.2 2.4 maximum_convert_fusion
  467.5 39.0 %reduce-scatter.3.cloned.1.call-done = bf16[64,1024]{1,0:T(8,128)(2,1)} async-done(((bf16[2048,1024]{1,0:T(8,128)(2,1)}), bf16[64,1024]{1,0:T(8,128)(2,1)}) %reduce-scatter.3.cloned.1.call-update) | async-done | bytes 131088 | tf_op jit(solution)/shard_map/reduce_scatter | solution.py:1068
  506.5 0.9 convert_element_type.21
  507.5 0.6 slice_bitcast_fusion.10
  508.1 0.7 maximum_bitcast_fusion.1
  508.8 148.4 %reduce-scatter.5.cloned.1.call-done = bf16[64,2048]{1,0:T(8,128)(2,1)} async-done(((bf16[2048,2048]{1,0:T(8,128)(2,1)}), bf16[64,2048]{1,0:T(8,128)(2,1)}) %reduce-scatter.5.cloned.1.call-update) | async-done | bytes 262160 | tf_op jit(solution)/shard_map/reduce_scatter | solution.py:1068
  657.2 1.0 convert_element_type.22
  658.2 0.8 slice_bitcast_fusion.8
  (58 shorter events, 0.5 us)
Async XLA Ops:
  7.2 37.5 %copy-start = (s32[4,1]{0,1:T(1,128)S(1)}, s32[4,1]{0,1:T(1,128)}, u32[]{:S(2)}) copy-start(s32[4,1]{0,1:T(1,128)} %param.31) | copy-start | bytes 52
  7.2 69.6 %all-gather.5.cloned.1.call-start = ((), (), s32[]{:S(2)}) async-start(), calls=%async_computation.2 | async-start | bytes 4325376 | tf_op jit(solution)/shard_map/all_gather | solution.py:1002
  9.5 146.7 %all-gather.7.cloned.1.call-start = ((), (), s32[]{:S(2)}) async-start(), calls=%async_computation.3 | async-start | bytes 8650752 | tf_op jit(solution)/shard_map/all_gather | solution.py:1002
  11.3 495.3 %reduce-scatter.3.cloned.1.call-start = ((), (), s32[]{:S(2)}) async-start(), calls=%async_computation.4 | async-start | bytes 4325376 | tf_op jit(solution)/shard_map/reduce_scatter | solution.py:1068
  11.3 4.6 copy-start.6
  11.3 5.0 copy-start.9
  11.3 5.0 copy-start.10
  11.4 5.0 copy-start.11
  11.4 5.0 copy-start.12
  11.4 5.0 copy-start.13
  11.4 5.0 copy-start.14
  11.4 5.1 copy-start.15
  11.4 5.1 copy-start.16
  11.4 5.1 copy-start.8
  12.8 33.1 %collective-permute-start = (bf16[512,512]{1,0:T(8,128)(2,1)S(1)}, bf16[512,512]{1,0:T(8,128)(2,1)S(1)}, u32[]{:S(2)}, u32[]{:S(2)}) collective-permute-start(bf16[512,512]{1,0:T(8,128)(2,1)S(1)} %get-tuple-element.90), channel_id=1, source_target_pairs={{0,1},{1,0},{2,3},{3,2},{4,5},{5,4},{6,7},{7,6},{8,9},{9,8},{10,11... | collective-permute-start | bytes 1572872 | tf_op jit(solution)/shard_map/ppermute | solution.py:997
  16.0 31.4 %collective-permute-start.4 = (bf16[512,512]{1,0:T(8,128)(2,1)S(1)}, bf16[512,512]{1,0:T(8,128)(2,1)S(1)}, u32[]{:S(2)}, u32[]{:S(2)}) collective-permute-start(bf16[512,512]{1,0:T(8,128)(2,1)S(1)} %get-tuple-element.80), channel_id=1, source_target_pairs={{0,1},{1,0},{2,3},{3,2},{4,5},{5,4},{6,7},{7,6},{8,9},{9,8},{10,11... | collective-permute-start | bytes 1572872 | tf_op jit(solution)/shard_map/ppermute | solution.py:997
  364.5 292.8 %reduce-scatter.5.cloned.1.call-start = ((), (), s32[]{:S(2)}) async-start(), calls=%async_computation.5 | async-start | bytes 8650752 | tf_op jit(solution)/shard_map/reduce_scatter | solution.py:1068
  364.5 1.2 copy-start.4
  364.5 1.5 copy-start.5
  366.5 4.5 copy-start.2
  366.5 4.5 copy-start.3
  367.5 78.0 %collective-permute-start.5 = (bf16[512,512]{1,0:T(8,128)(2,1)}, bf16[512,512]{1,0:T(8,128)(2,1)S(1)}, u32[]{:S(2)}, u32[]{:S(2)}) collective-permute-start(bf16[512,512]{1,0:T(8,128)(2,1)} %get-tuple-element.78), channel_id=1, source_target_pairs={{0,1},{1,0},{16,17},{17,16},{2,3},{3,2},{18,19},{19,18},{4,5},{5,4... | collective-permute-start | bytes 1572872 | tf_op jit(solution)/shard_map/ppermute | solution.py:981
  368.9 80.3 %collective-permute-start.6 = (bf16[512,512]{1,0:T(8,128)(2,1)S(1)}, bf16[512,512]{1,0:T(8,128)(2,1)S(1)}, u32[]{:S(2)}, u32[]{:S(2)}) collective-permute-start(bf16[512,512]{1,0:T(8,128)(2,1)S(1)} %get-tuple-element.77), channel_id=1, source_target_pairs={{0,16},{1,17},{16,0},{17,1},{2,18},{3,19},{18,2},{19,3},{4,20},{5,... | collective-permute-start | bytes 1572872 | tf_op jit(solution)/shard_map/ppermute | solution.py:981
  369.5 79.7 %collective-permute-start.7 = (bf16[512,512]{1,0:T(8,128)(2,1)S(1)}, bf16[512,512]{1,0:T(8,128)(2,1)}, u32[]{:S(2)}, u32[]{:S(2)}) collective-permute-start(bf16[512,512]{1,0:T(8,128)(2,1)S(1)} %get-tuple-element.76), channel_id=1, source_target_pairs={{0,17},{1,16},{16,1},{17,0},{2,19},{3,18},{18,3},{19,2},{4,21},{5,... | collective-permute-start | bytes 1572872 | tf_op jit(solution)/shard_map/ppermute | solution.py:981
  371.4 3.3 copy-start.7
  372.6 78.1 %collective-permute-start.1 = (bf16[512,512]{1,0:T(8,128)(2,1)}, bf16[512,512]{1,0:T(8,128)(2,1)}, u32[]{:S(2)}, u32[]{:S(2)}) collective-permute-start(bf16[512,512]{1,0:T(8,128)(2,1)} %get-tuple-element.88), channel_id=1, source_target_pairs={{0,1},{1,0},{16,17},{17,16},{2,3},{3,2},{18,19},{19,18},{4,5},{5,4... | collective-permute-start | bytes 1572872 | tf_op jit(solution)/shard_map/ppermute | solution.py:981
  374.1 76.6 %collective-permute-start.2 = (bf16[512,512]{1,0:T(8,128)(2,1)}, bf16[512,512]{1,0:T(8,128)(2,1)}, u32[]{:S(2)}, u32[]{:S(2)}) collective-permute-start(bf16[512,512]{1,0:T(8,128)(2,1)} %get-tuple-element.87), channel_id=1, source_target_pairs={{0,16},{1,17},{16,0},{17,1},{2,18},{3,19},{18,2},{19,3},{4,20},{5,... | collective-permute-start | bytes 1572872 | tf_op jit(solution)/shard_map/ppermute | solution.py:981
  445.4 16.5 %collective-permute-start.3 = (bf16[512,512]{1,0:T(8,128)(2,1)}, bf16[512,512]{1,0:T(8,128)(2,1)S(1)}, u32[]{:S(2)}, u32[]{:S(2)}) collective-permute-start(bf16[512,512]{1,0:T(8,128)(2,1)} %get-tuple-element.86), channel_id=1, source_target_pairs={{0,17},{1,16},{16,1},{17,0},{2,19},{3,18},{18,3},{19,2},{4,21},{5,... | collective-permute-start | bytes 1572872 | tf_op jit(solution)/shard_map/ppermute | solution.py:981
  465.2 193.9 %copy-start.1 = (s32[4,1]{0,1:T(1,128)S(1)}, s32[4,1]{0,1:T(1,128)}, u32[]{:S(2)}) copy-start(s32[4,1]{0,1:T(1,128)} %param.31) | copy-start | bytes 52
Sparse Core Ops, SparseCore 0:
  11.6 65.0 all-gather.4
  80.3 75.8 all-gather.6
  364.6 141.8 reduce-scatter.2
  508.7 148.5 reduce-scatter.4
